TPU v7x, 512 devices: a whole 4x8x8 slice. The times are simulated.
512 devices in a mesh: space: 64 (over z, y), term: 8 (over x, core).
Axes of the slice: x: 4, y: 8, z: 8, core: 2. Of those that a mesh axis runs over, the one named last changes fastest.
Arguments:
- x_modes: bfloat16 [64, 512], P('space'), may hold values from -0.125 to 0.125
- y_modes: bfloat16 [32, 512], replicated, may hold values from -5 to 5
- z_modes: bfloat16 [512, 128], replicated, may hold values from -5 to 5
- coefficients: float32 [64, 512], P('term'), may hold values from -5 to 5
- magic_cells: int32 [32], replicated, may hold values from 0 to 262143
- interp_inverse: float32 [32, 32], replicated, may hold values from -1 to 1, as said below
- eim_basis: bfloat16 [32, 262144], P('term', 'space'), may hold values from 0.006225586 to 0.0625
- basis: bfloat16 [96, 262144], P(None, 'space'), may hold values from -0.013621858 to 0.013621858
Outputs:
- eim_coefficients: float32 [32, 64], P(None, 'term')
- interp_error: bfloat16 [64, 262144], P('term', 'space')
- term_operators: float32 [32, 9216], P('term', 'space')
- assembled: float32 [64, 9216], P('term', 'space')
Inputs may be any that keep to these rules, and one draw needn't show every extreme that they name: `interp_inverse`: lower triangular with ones on the diagonal.
All inputs are finite; a program needn't handle non-finite values.
Results may differ from a plain program's by a relative error of at most 0.0015.
The roundings to bfloat16 on the way count: a program that leaves them out, or rounds other values in their place, can miss the bound.
Values may be sent and summed in bfloat16 or wider, within the bound.
No kernel may reach another device: no remote copies, remote signals or barrier semaphores. Data moves between devices by JAX's collectives and lax.ppermute only.
A program may use at most 64 MiB of HBM per device.

v0:
```python
import jax
import jax.numpy as jnp
from jax import lax
from jax.sharding import PartitionSpec as P


def shifted(array, axis, by):
    size = lax.axis_size(axis)
    pairs = [(i, i + by) for i in range(size) if 0 <= i + by < size]
    return lax.ppermute(array, axis, pairs)


def differences(stacked):
    widened = stacked.astype(jnp.float32)
    current = widened[:, :-1]
    along_x = widened[:, 1:] - current
    zeros_y = jnp.zeros_like(current[:, :, :1])
    along_y = jnp.concatenate([current[:, :, 1:], zeros_y], 2) - current
    zeros_z = jnp.zeros_like(current[:, :, :, :1])
    along_z = jnp.concatenate([current[:, :, :, 1:], zeros_z], 3) - current
    row_count = current.shape[0]
    return [
        part_diff.astype(jnp.bfloat16).reshape(row_count, -1)
        for part_diff in (along_x, along_y, along_z)
    ]


def weighted_gram(diff_list, weights):
    summed = None
    for difference in diff_list:
        weighted = (
            weights.astype(jnp.float32)[:, None, :] * difference.astype(jnp.float32)[None]
        ).astype(jnp.bfloat16)
        weighted = weighted.reshape(-1, difference.shape[1])
        product = lax.dot_general(
            difference, weighted, (((1,), (1,)), ((), ())), preferred_element_type=jnp.float32
        )
        summed = product if summed is None else summed + product
    return summed


def local(x_modes, y_modes, z_modes, coefficients, magic_cells, interp_inverse, eim_basis, basis):
    planes = x_modes.shape[0]
    width_y = y_modes.shape[0]
    width_z = z_modes.shape[1]
    plane_size = width_y * width_z
    cell_dev = planes * plane_size
    snap_count = coefficients.shape[0]
    rank = basis.shape[0]
    term_dev = eim_basis.shape[0]
    space_index = lax.axis_index("space")
    space_count = lax.axis_size("space")
    basis_grid = basis.reshape(rank, planes, width_y, width_z)
    following = shifted(basis_grid[:, 0], "space", -1)
    stacked = jnp.concatenate([basis_grid, following[:, None]], 1)
    summed = weighted_gram(differences(stacked), eim_basis)
    scaled = x_modes.astype(jnp.float32)[None, :, None, :] * coefficients[:, None, None, :]
    left_factor = (scaled * y_modes.astype(jnp.float32)[None, None, :, :]).astype(jnp.bfloat16)
    log_field = jnp.dot(
        left_factor.reshape(-1, left_factor.shape[-1]), z_modes, preferred_element_type=jnp.float32
    )
    conductivity = jnp.exp(log_field.reshape(snap_count, cell_dev))
    local_cell = magic_cells - space_index * cell_dev
    inside_cell = (local_cell >= 0) & (local_cell < cell_dev)
    picked = jnp.take(conductivity, jnp.clip(local_cell, 0, cell_dev - 1), axis=1)
    sample_values = lax.psum(jnp.where(inside_cell[None, :], picked, 0.0), "space")
    eim_coefficients = jnp.dot(interp_inverse, sample_values.T, precision=lax.Precision.HIGHEST)
    rounded = eim_coefficients.astype(jnp.bfloat16)
    fitted = lax.dot_general(
        rounded,
        lax.all_gather(eim_basis, "term", axis=0, tiled=True),
        (((0,), (0,)), ((), ())),
        preferred_element_type=jnp.float32,
    )
    interp_error = (conductivity - fitted).astype(jnp.bfloat16)
    partial_ops = (
        summed.reshape(rank, term_dev, rank).transpose(1, 0, 2).reshape(term_dev, rank * rank)
    )
    share_width = rank * rank // space_count
    full_ops = lax.psum(partial_ops, "space")
    term_operators = lax.dynamic_slice_in_dim(full_ops, space_index * share_width, share_width, 1)
    all_operators = lax.all_gather(term_operators, "term", axis=0, tiled=True)
    assembled = jnp.dot(eim_coefficients.T, all_operators, precision=lax.Precision.HIGHEST)
    return (eim_coefficients, interp_error, term_operators, assembled)


def solution(mesh):
    placed = (
        P("space", None),
        P(),
        P(),
        P("term", None),
        P(),
        P(),
        P("term", "space"),
        P(None, "space"),
    )
    return jax.shard_map(
        local,
        mesh=mesh,
        in_specs=placed,
        out_specs=(P(None, "term"), P("term", "space"), P("term", "space"), P("term", "space")),
        check_vma=False,
    )
```

profile of v0, /device:TPU:1, one launch (start us, length us, event | category | flops | bytes accessed | tf_op | source)
XLA Modules:
  0.0 494.3 jit_solution(5528251816082864872)
XLA Ops:
  7.2 0.0 copy-start
  7.2 0.0 copy-start.1
  7.2 0.0 copy-start.4
  7.2 0.0 copy-start.3
  7.2 0.0 all-reduce.4.cloned.1.call-start
  7.3 1.3 copy.16
  8.6 1.3 collective-permute-start
  9.9 0.8 convert_element_type.103
  10.7 0.8 convert_element_type.96
  11.4 0.7 mul.111
  12.1 0.7 broadcast_multiply_fusion
  12.9 0.0 copy-done
  12.9 0.2 convolution_exponential_fusion
  13.1 0.6 copy.14
  13.7 0.0 copy-done.1
  13.8 20.6 %all-gather = bf16[8,4,4096]{2,1,0:T(4,128)(2,1)} all-gather(bf16[1,4,4096]{2,1,0:T(4,128)(2,1)S(1)} %bitcast.64), channel_id=1, replica_groups=mesh['space'=64,'term'=8] {'term'}, dimensions={0}, use_global_device_ids=true | all-gather | bytes 294912 | tf_op jit(solution)/shard_map/all_gather | solution.py:71
  34.4 1.0 reshape.124
  35.4 0.0 copy-done.4
  35.5 0.6 gather_fusion
  36.0 0.1 select_bitcast_fusion
  36.1 228.9 %psum.14 = f32[8,32]{0,1:T(8,128)S(1)} all-reduce(f32[8,32]{0,1:T(8,128)S(1)} %select_bitcast_fusion), channel_id=1, replica_groups=mesh['space'=64,'term'=8] {'space'}, use_global_device_ids=true, to_apply=%region_0.1 | all-reduce | flops 256 | bytes 2048 | tf_op jit(solution)/shard_map/psum | solution.py:66
  265.0 0.0 copy-done.3
  265.0 0.2 fusion.10
  265.2 0.0 copy-start.2
  265.2 0.0 collective-permute-done
  265.2 1.4 maximum_convert_fusion
  266.6 0.2 slice.22
  266.8 0.5 slice.23
  267.3 0.8 subtract_convert_fusion
  268.1 0.3 bitcast_convert_fusion.2
  268.3 0.7 bitcast_convert_fusion
  269.0 2.1 multiply_convert_fusion
  271.1 1.1 fusion.4
  272.2 1.1 convolution_add_fusion.1
  273.2 1.1 convolution_add_fusion
  274.3 0.2 reshape.111
  274.5 0.8 reshape.112
  275.4 0.0 all-reduce.4.cloned.1.call-update
  275.4 0.8 fusion
  276.2 190.5 %all-reduce.4.cloned.1.call-done = f32[4,9216]{1,0:T(4,128)} async-done(((f32[4,9216]{1,0:T(4,128)}), f32[4,9216]{1,0:T(4,128)}) %all-reduce.4.cloned.1.call-update) | async-done | bytes 147472 | tf_op jit(solution)/shard_map/psum | solution.py:80
  466.7 0.8 fusion.22
  467.4 17.9 %all-gather.1 = f32[8,4,144]{2,1,0:T(4,128)S(1)} all-gather(f32[1,4,144]{2,1,0:T(4,128)S(1)} %fusion.22), channel_id=1, replica_groups=mesh['space'=64,'term'=8] {'term'}, dimensions={0}, use_global_device_ids=true | all-gather | bytes 20736 | tf_op jit(solution)/shard_map/all_gather | solution.py:82
  485.3 0.0 copy-done.2
  485.3 0.7 fusion.11
  486.1 1.4 constant_dynamic-slice_fusion
  (6 shorter events, 0.1 us)
Async XLA Ops:
  7.2 5.7 %copy-start = (bf16[512,128]{1,0:T(8,128)(2,1)S(1)}, bf16[512,128]{1,0:T(8,128)(2,1)}, u32[]{:S(2)}) copy-start(bf16[512,128]{1,0:T(8,128)(2,1)} %param.10) | copy-start | bytes 393220
  7.2 6.6 %copy-start.1 = (bf16[4,4096]{1,0:T(4,128)(2,1)S(1)}, bf16[4,4096]{1,0:T(4,128)(2,1)}, u32[]{:S(2)}) copy-start(bf16[4,4096]{1,0:T(4,128)(2,1)} %param.14) | copy-start | bytes 98308
  7.2 28.2 %copy-start.4 = (s32[32]{0:T(128)S(1)}, s32[32]{0:T(128)}, u32[]{:S(2)}) copy-start(s32[32]{0:T(128)} %param.12) | copy-start | bytes 388
  7.2 257.8 %copy-start.3 = (f32[32,32]{1,0:T(8,128)S(1)}, f32[32,32]{1,0:T(8,128)}, u32[]{:S(2)}) copy-start(f32[32,32]{1,0:T(8,128)} %param.13) | copy-start | bytes 12292
  7.2 459.4 %all-reduce.4.cloned.1.call-start = ((), (), s32[]{:S(2)}) async-start(), calls=%async_computation | async-start | bytes 294912 | tf_op jit(solution)/shard_map/psum | solution.py:80
  8.6 256.6 %collective-permute-start = (bf16[96,32,128]{2,1,0:T(8,128)(2,1)S(1)}, bf16[96,32,128]{2,1,0:T(8,128)(2,1)}, u32[]{:S(2)}, u32[]{:S(2)}) collective-permute-start(bf16[96,32,128]{2,1,0:T(8,128)(2,1)S(1)} %bitcast.59), channel_id=1, source_target_pairs={{8,0},{16,8},{24,16},{32,24},{40,32},{48,40},{56,48},{64,56},{72,6... | collective-permute-start | bytes 2359304 | tf_op jit(solution)/shard_map/ppermute | solution.py:10
  265.2 220.1 %copy-start.2 = (f32[8,32]{1,0:T(8,128)}, f32[8,32]{1,0:T(8,128)S(1)}, u32[]{:S(2)}) copy-start(f32[8,32]{1,0:T(8,128)S(1)} %fusion.10) | copy-start | bytes 3076
Sparse Core Ops, SparseCore 0:
  275.5 191.0 all-reduce.3
where the time goes:
time: 495 us; the launch traced here: 494 us
  blocking collectives  267 us (54%)
  waiting for transfers between devices  190 us (38%)
  between operations  14.2 us (3%)
  other arithmetic  8.19 us (2%)
  local copies, waits for them, and re-layouts  7.41 us (1%)
  matrix products  5.19 us (1%)
    psum x1, blocking collectives, local(): lax.psum(jnp.where(inside_cell[None, :], picked, 0.0), 'space')  229 us
    psum x1, waiting for transfers between devices, local(): full_ops = lax.psum(partial_ops, 'space')  190 us
    all_gather x1, blocking collectives, local(): lax.all_gather(eim_basis, 'term', axis=0, tiled=True)  20.6 us
    all_gather x1, blocking collectives, local(): all_operators = lax.all_gather(term_operators, 'term', axis=0, tiled=True)  17.9 us
  transfers between devices with their start and end apart: 2, of which 1 were waited for; matrix products, arithmetic and copies ran while one was open for 1% of the time, Pallas kernels for 0%

commit v1 on v0

v1 whole, which is shorter than its diff:
```python
import jax
import jax.numpy as jnp
from jax import lax
from jax.experimental import pallas as pl
from jax.experimental.pallas import tpu as pltpu
from jax.sharding import PartitionSpec as P

F32, BF16 = jnp.float32, jnp.bfloat16
VMEM = pl.BlockSpec(memory_space=pltpu.VMEM)
SMEM = pl.BlockSpec(memory_space=pltpu.SMEM)
CHUNK = 512
EXACT = lax.Precision.HIGHEST


def call(body, out_shape, inputs, specs=None, scratch=(), flops=0, moved=0):
    return pl.pallas_call(
        body,
        out_shape=out_shape,
        in_specs=specs or [VMEM] * len(inputs),
        out_specs=jax.tree.map(lambda _: VMEM, out_shape),
        scratch_shapes=list(scratch),
        compiler_params=pltpu.CompilerParams(vmem_limit_bytes=32 << 20),
        cost_estimate=pl.CostEstimate(flops=flops, bytes_accessed=moved, transcendentals=0),
    )(*inputs)


def gram_of(diff, weights):
    rank, cells = diff.shape
    blocks = diff.reshape(rank // 16, 16, cells)
    weighted = []
    for q in range(weights.shape[0]):
        row = jnp.broadcast_to(weights[q : q + 1], (16, cells)).astype(BF16)
        weighted.append((blocks * row[None]).reshape(rank, cells))
    half = rank // 2
    ordered = [w[:half] for w in weighted] + [w[half:] for w in weighted]
    return lax.dot_general(
        jnp.concatenate(ordered, 0), diff, (((1,), (1,)), ((), ())), preferred_element_type=F32
    )


def inner_gram(width_z, basis_ref, eim_ref, out_ref):
    rank, cells = basis_ref.shape
    last = lax.broadcasted_iota(jnp.int32, (rank, width_z), 1) == width_z - 1
    total = jnp.zeros(out_ref.shape, F32)
    for start in range(0, cells, CHUNK):
        current = basis_ref[:, start : start + CHUNK].astype(F32)
        if start + CHUNK < cells:
            after = basis_ref[:, start + width_z : start + CHUNK + width_z].astype(F32)
        else:
            after = jnp.concatenate([current[:, width_z:], jnp.zeros((rank, width_z), F32)], 1)
        weights = eim_ref[:, start : start + CHUNK].astype(F32)
        total += gram_of((after - current).astype(BF16), weights)
        pieces = []
        for at in range(0, CHUNK, width_z):
            piece = current[:, at : at + width_z]
            moved = jnp.where(last, 0.0, pltpu.roll(piece, width_z - 1, 1))
            pieces.append((moved - piece).astype(BF16))
        total += gram_of(jnp.concatenate(pieces, 1), weights)
    out_ref[...] = total


def own_half(side_ref, basis_ref, out_ref):
    del side_ref
    out_ref[...] = basis_ref[...]


def outer_gram(ranks, side_ref, basis_ref, following_ref, eim_ref, inner_ref, x_ref, out_ref):
    half = following_ref.shape[1]
    depth = inner_ref.shape[0] // 2
    total = []
    for at in (0, depth):
        own = inner_ref[at : at + depth]
        total += [jnp.where(side_ref[0] == 0, own, 0.0), jnp.where(side_ref[0] == 0, 0.0, own)]
    total = jnp.concatenate(total, 0)
    for start in range(0, half, CHUNK):
        part = pl.ds(pl.multiple_of(side_ref[0] * half + start, CHUNK), CHUNK)
        after = following_ref[:, start : start + CHUNK].astype(F32)
        diff = (after - basis_ref[:, part].astype(F32)).astype(BF16)
        total += gram_of(diff, eim_ref[:, part].astype(F32))
    rows = total.T
    width = rows.shape[1]
    modes = x_ref[...].astype(F32)
    fill = jnp.zeros((1, out_ref.shape[2] - width), F32)
    for place, share in enumerate(ranks):
        at = 3 * (share // 2)
        if share % 2 == 0:
            whole, part = rows[at : at + 1], rows[at + 1 : at + 2, : width // 2]
        else:
            whole, part = rows[at + 2 : at + 3], rows[at + 1 : at + 2, width // 2 :]
        whole = jnp.concatenate([whole, fill], 1)
        part = jnp.concatenate([part, modes], 1)
        out_ref[place] = jnp.concatenate([whole, part], 0).astype(BF16)


def in_order(odd_ref, own_ref, other_ref, out_ref):
    own, other = own_ref[...].astype(F32), other_ref[...].astype(F32)
    even = odd_ref[0] == 0
    first, second = jnp.where(even, own, other), jnp.where(even, other, own)
    out_ref[...] = jnp.concatenate([first, second], 0).astype(BF16)


def two_cores(core_ref, own_ref, other_ref, out_ref):
    own, other = own_ref[...].astype(F32), other_ref[...].astype(F32)
    even = core_ref[0] == 0
    first, second = jnp.where(even, own, other), jnp.where(even, other, own)
    terms = own.shape[0] // 2
    rows = [first[:terms], second[:terms], first[terms:], second[terms:]]
    out_ref[...] = jnp.concatenate(rows, 0).astype(BF16)


def field(
    cells_ref, x_ref, y_ref, z_ref, coefficients_ref, at_y_ref, at_z_ref, conductivity_ref, pick_z, wide_y
):
    width_y, width_z = y_ref.shape[0], z_ref.shape[1]
    plane = width_y * width_z
    wide_y[...] = y_ref[...].astype(F32)
    lanes = lax.broadcasted_iota(jnp.int32, (1, width_z), 1)
    for q in range(cells_ref.shape[0]):
        cell = cells_ref[q]
        at_y_ref[q : q + 1] = wide_y[pl.ds((cell % plane) // width_z, 1), :]
        pick_z[q : q + 1] = jnp.where(lanes == cell % width_z, 1.0, 0.0)
    at_z_ref[...] = lax.dot_general(
        pick_z[...].astype(BF16), z_ref[...], (((1,), (1,)), ((), ())), preferred_element_type=F32
    )
    scaled = x_ref[...].astype(F32) * coefficients_ref[...]
    left = [(scaled * wide_y[y : y + 1]).astype(BF16) for y in range(width_y)]
    logs = jnp.dot(jnp.concatenate(left, 0), z_ref[...], preferred_element_type=F32)
    conductivity_ref[...] = jnp.exp(logs)


def interpolation(
    meet, plane, cells_ref, chip_ref, arrived_ref, at_y_ref, at_z_ref, conductivity_ref,
    coefficients_ref, inverse_ref, near_eim_ref, far_eim_ref, turned_ref, kept_ref, error_ref, pick_x,
):
    points, modes = pick_x.shape
    slabs = arrived_ref.shape[0]
    snaps = coefficients_ref.shape[0]
    width_z = conductivity_ref.shape[1]
    gram_width = arrived_ref.shape[2] - modes
    for q in range(points):
        slab = (cells_ref[q] // plane + slabs - meet) % slabs
        pick_x[q : q + 1] = arrived_ref[slab][:, gram_width:].astype(F32)[1:2]
    at_x, at_y, at_z = pick_x[...], at_y_ref[...], at_z_ref[...]
    coefficients = coefficients_ref[...]
    lane = lax.broadcasted_iota(jnp.int32, (points, 128), 1)
    logs = jnp.zeros((points, 128), F32)
    for s in range(snaps):
        left = ((at_x * coefficients[s : s + 1]) * at_y).astype(BF16).astype(F32)
        logs += jnp.where(lane == s, jnp.sum(left * at_z, axis=1, keepdims=True), 0.0)
    samples = jnp.exp(logs)
    values = jnp.dot(inverse_ref[...], samples, precision=EXACT, preferred_element_type=F32)
    turned = values.T[:snaps]
    turned_ref[...] = turned
    kept_ref[...] = turned
    depth = near_eim_ref.shape[0]
    swapped = jnp.concatenate([turned[:, depth:], turned[:, :depth]], 1)
    rounded = jnp.where(chip_ref[0] // 2 == 0, turned, swapped).astype(BF16)
    basis = jnp.concatenate([near_eim_ref[...], far_eim_ref[...]], 0)
    fitted = jnp.dot(rounded, basis, preferred_element_type=F32)
    for y in range(plane // width_z):
        part = slice(y * width_z, (y + 1) * width_z)
        error = conductivity_ref[y * snaps : (y + 1) * snaps] - fitted[:, part]
        error_ref[:, part] = error.astype(BF16)


def own_share(rank, odd_ref, arrived_ref, spread_ref):
    terms = spread_ref.shape[1]
    width = terms * rank
    half = rank // 2
    total = jnp.sum(arrived_ref[:, :, :width].astype(F32), axis=0)
    whole, part = total[0:1], total[1:2, : width // 2]
    odd = odd_ref[0] == 1
    picked = []
    for q in range(terms):
        first = whole[:, q * half : (q + 1) * half]
        second = whole[:, width // 2 + q * half : width // 2 + (q + 1) * half]
        single = part[:, q * half : (q + 1) * half]
        even_form = jnp.concatenate([first, second, single], 1)
        odd_form = jnp.concatenate([single, first, second], 1)
        picked.append(jnp.where(odd, odd_form, even_form))
    own = jnp.concatenate(picked, 0)
    for t in range(spread_ref.shape[0]):
        spread_ref[t] = own


def assembly(turn, core_ref, chip_ref, turned_ref, operators_ref, own_ref, out_ref):
    turned = turned_ref[...]
    count, both = operators_ref.shape[:2]
    terms = both // 2
    total = jnp.zeros(out_ref.shape, F32)
    for first in (0, 1, 4, 5):
        at = (first + count - turn) % count
        block = operators_ref[at] + operators_ref[at + 2]
        for j in range(both):
            q = (first + 2 * (j // terms)) * terms + j % terms
            total += turned[:, q : q + 1] * block[j : j + 1]
    out_ref[...] = total
    at = (4 * (chip_ref[0] // 2) + core_ref[0] + count - turn) % count
    own = operators_ref[at] + operators_ref[at + 2]
    own_ref[...] = jnp.where(chip_ref[0] % 2 == 0, own[:terms], own[terms:])


def local(x_modes, y_modes, z_modes, coefficients, magic_cells, interp_inverse, eim_basis, basis):
    space, term = "space", "term"
    slabs, groups = lax.axis_size(space), lax.axis_size(term)
    modes = x_modes.shape[1]
    width_y, width_z = y_modes.shape[0], z_modes.shape[1]
    snaps, points = coefficients.shape[0], magic_cells.shape[0]
    rank, cells = basis.shape
    terms = eim_basis.shape[0]
    share = rank * rank // slabs
    shape = jax.ShapeDtypeStruct

    slab = lax.axis_index(space).astype(jnp.int32).reshape(1)
    place = lax.axis_index(term).astype(jnp.int32).reshape(1)
    core, chip = place % 2, place // 2
    side = chip % 2
    half = cells // 2
    meet, turn = slabs // 2 + slabs // 16, groups // 2
    ranks = [(meet + i) % slabs for i in range(slabs)]
    term_ranks = [(turn + i) % groups for i in range(groups)]
    swap = [(i, i ^ 1) for i in range(groups)]
    mine = pl.pallas_call(
        own_half,
        out_shape=shape((rank, half), BF16),
        grid_spec=pltpu.PrefetchScalarGridSpec(
            num_scalar_prefetch=1,
            grid=(1,),
            in_specs=[pl.BlockSpec((rank, half), lambda i, side_ref: (0, side_ref[0]))],
            out_specs=pl.BlockSpec((rank, half), lambda i, side_ref: (0, 0)),
        ),
        compiler_params=pltpu.CompilerParams(vmem_limit_bytes=32 << 20),
        cost_estimate=pl.CostEstimate(flops=0, bytes_accessed=2 * basis.size, transcendentals=0),
    )(side, basis)
    near = lax.ppermute(mine, space, [(i + 1, i) for i in range(slabs - 1)])
    eim_beside = lax.ppermute(eim_basis, term, [(i, i ^ 2) for i in range(groups)])
    gram_flops = 2 * rank * rank * terms * cells
    inner = call(
        lambda *refs: inner_gram(width_z, *refs),
        shape((terms * rank, rank), F32),
        (basis, eim_basis),
        flops=2 * gram_flops,
        moved=2 * basis.size,
    )
    eim_beside, inner = lax.optimization_barrier((eim_beside, inner))
    eim_pair = call(
        in_order,
        shape((2 * terms, cells), BF16),
        (side, eim_basis, eim_beside),
        specs=[SMEM, VMEM, VMEM],
        moved=8 * eim_basis.size,
    )
    eim_other = lax.ppermute(eim_pair, term, swap)
    near, inner, eim_pair = lax.optimization_barrier((near, inner, eim_pair))
    packed = call(
        lambda *refs: outer_gram(ranks, *refs),
        shape((slabs, 2, terms * rank + modes), BF16),
        (side, basis, near, eim_pair, inner, x_modes),
        specs=[SMEM] + [VMEM] * 5,
        flops=gram_flops,
        moved=4 * basis.size,
    )
    packed, eim_other, factors = lax.optimization_barrier((packed, eim_other, coefficients))
    eim_near = call(
        two_cores,
        shape((4 * terms, cells), BF16),
        (core, eim_pair, eim_other),
        specs=[SMEM, VMEM, VMEM],
        moved=16 * eim_basis.size,
    )
    eim_far = lax.ppermute(eim_near, term, [(i, i ^ (groups - 2)) for i in range(groups)])
    arrived = lax.all_to_all(packed, space, 0, 0, axis_index_groups=[ranks], tiled=True)
    at_y, at_z, conductivity = call(
        field,
        (
            shape((points, modes), F32),
            shape((points, modes), F32),
            shape((width_y * snaps, width_z), F32),
        ),
        (magic_cells, x_modes, y_modes, z_modes, factors),
        specs=[SMEM] + [VMEM] * 4,
        scratch=[pltpu.VMEM((points, width_z), F32), pltpu.VMEM((width_y, modes), F32)],
        flops=2 * snaps * width_y * modes * width_z,
        moved=4 * points * cells,
    )
    arrived, at_y, at_z, conductivity = lax.optimization_barrier(
        (arrived, at_y, at_z, conductivity)
    )
    eim_turned, turned, interp_error = call(
        lambda *refs: interpolation(meet, cells, *refs),
        (shape((snaps, points), F32), shape((snaps, points), F32), shape((snaps, cells), BF16)),
        (magic_cells, chip, arrived, at_y, at_z, conductivity, coefficients, interp_inverse)
        + (eim_near, eim_far),
        specs=[SMEM] * 2 + [VMEM] * 8,
        scratch=[pltpu.VMEM((points, modes), F32)],
        flops=2 * snaps * points * cells,
        moved=4 * points * cells,
    )
    odd = slab % 2
    spread = call(
        lambda *refs: own_share(rank, *refs),
        shape((groups, 2 * terms, share), F32),
        (odd, arrived),
        specs=[SMEM, VMEM],
        moved=4 * packed.size,
    )
    all_operators = lax.all_to_all(spread, term, 0, 0, axis_index_groups=[term_ranks], tiled=True)
    term_operators, assembled = call(
        lambda *refs: assembly(turn, *refs),
        (shape((terms, share), F32), shape((snaps, share), F32)),
        (core, chip, turned, all_operators),
        specs=[SMEM, SMEM, VMEM, VMEM],
        moved=1 << 15,
    )
    return (eim_turned.T, interp_error, term_operators, assembled)


def solution(mesh):
    space, term = "space", "term"
    placed = (
        P(space, None),
        P(),
        P(),
        P(term, None),
        P(),
        P(),
        P(term, space),
        P(None, space),
    )
    return jax.shard_map(
        local,
        mesh=mesh,
        in_specs=placed,
        out_specs=(P(None, term), P(term, space), P(term, space), P(term, space)),
        check_vma=False,
    )
```

time: 495 us -> 54.5 us (0.11)
  blocking collectives: 267 us -> 0 us
  waiting for transfers between devices: 190 us -> 0.2 us
  starting transfers between devices: 1.33 us -> 42.7 us
  between operations: 14.2 us -> 0.88 us
  Pallas kernels: 0 us -> 8.53 us
  other arithmetic: 8.19 us -> 0 us
  local copies, waits for them, and re-layouts: 7.41 us -> 1.78 us
  matrix products: 5.19 us -> 0 us
    psum x1 -> x0, blocking collectives: 229 us -> none  [local(): lax.psum(jnp.where(inside_cell[None, :], picked, 0.0), 'space')]
    psum x1 -> x0, waiting for transfers between devices: 190 us -> none  [local(): full_ops = lax.psum(partial_ops, 'space')]
    all_gather x2 -> x0, blocking collectives: 38.5 us -> none  [the longest x1 20.6 us: local(): lax.all_gather(eim_basis, 'term', axis=0, tiled=True)]
    all_to_all x0 -> x2, starting transfers between devices: none -> 24.2 us  [the longest x1 17.2 us: local(): lax.all_to_all(packed, space, 0, 0, axis_index_groups=[ranks], tiled=True)]
    ppermute x1 -> x4, starting transfers between devices: 1.29 us -> 18.5 us  [the longest x1 8.75 us: local(): eim_other = lax.ppermute(eim_pair, term, swap)]
    pallas_call x0 -> x9, Pallas kernels: none -> 8.53 us  [the longest x8 8.51 us: call(): pl.pallas_call(body, out_shape=out_shape, in_specs=specs or [VMEM] * len(...]
    convert_element_type x8 -> x0, other arithmetic: 6.69 us -> none  [the longest x1 2.05 us: weighted_gram(): weighted = (weights.astype(jnp.float32)[:, None, :] * difference.astype(j...]
    dot_general x7 -> x0, matrix products: 5.19 us -> none  [the longest x3 3.26 us: weighted_gram(): lax.dot_general(difference, weighted, (((1,), (1,)), ((), ())), preferred...]
  transfers between devices with their start and end apart: 2 -> 6, of which waited for: 1 -> 1; matrix products, arithmetic and copies ran while one was open for 1% -> 0% of each run, Pallas kernels for 0% -> 14%
where the time goes in v1:
time: 54.5 us; the launch traced here: 54.1 us
  starting transfers between devices  42.7 us (78%)
  Pallas kernels  8.53 us (16%)
  local copies, waits for them, and re-layouts  1.78 us (3%)
  between operations  0.88 us (2%)
    all_to_all x1, starting transfers between devices, local(): lax.all_to_all(packed, space, 0, 0, axis_index_groups=[ranks], tiled=True)  17.2 us
    ppermute x1, starting transfers between devices, local(): eim_other = lax.ppermute(eim_pair, term, swap)  8.75 us
    pallas_call x8, Pallas kernels, call(): pl.pallas_call(body, out_shape=out_shape, in_specs=specs or [VMEM] * len(...  8.51 us
    all_to_all x1, starting transfers between devices, local(): lax.all_to_all(spread, term, 0, 0, axis_index_groups=[term_ranks], tiled=...  6.97 us
    ppermute x1, starting transfers between devices, local(): lax.ppermute(eim_near, term, [(i, i ^ groups - 2) for i in range(groups)])  4.38 us
    ppermute x1, starting transfers between devices, local(): lax.ppermute(eim_basis, term, [(i, i ^ 2) for i in range(groups)])  3.95 us
    unnamed x18, local copies, waits for them, and re-layouts  1.78 us
    ppermute x1, starting transfers between devices, local(): near = lax.ppermute(mine, space, [(i + 1, i) for i in range(slabs - 1)])  1.42 us
  transfers between devices with their start and end apart: 6, of which 1 were waited for; matrix products, arithmetic and copies ran while one was open for 0% of the time, Pallas kernels for 14%

profile of v1, /device:TPU:1, one launch (start us, length us, event | category | flops | bytes accessed | tf_op | source)
XLA Modules:
  0.0 54.1 jit_solution(13350108465130518925)
XLA Ops:
  0.7 0.0 copy-start
  0.7 1.1 %copy-done = bf16[96,4096]{1,0:T(8,128)(2,1)S(1)} copy-done((bf16[96,4096]{1,0:T(8,128)(2,1)S(1)}, bf16[96,4096]{1,0:T(8,128)(2,1)}, u32[]{:S(2)}) %copy-start) | copy-done | bytes 786456
  1.8 0.0 copy-start.4
  1.8 0.0 copy-start.1
  1.8 1.4 %collective-permute-start = (bf16[96,2048]{1,0:T(8,128)(2,1)S(1)}, bf16[96,2048]{1,0:T(8,128)(2,1)S(1)}, u32[]{:S(2)}, u32[]{:S(2)}) collective-permute-start(bf16[96,2048]{1,0:T(8,128)(2,1)S(1)} %shard_map.111), channel_id=1, source_target_pairs={{8,0},{16,8},{24,16},{32,24},{40,32},{48,40},{56,48},{64,56},{72,6... | collective-permute-start | bytes 1179656 | tf_op jit(solution)/shard_map/ppermute | solution.py:235
  3.3 0.0 copy-done.4
  3.3 3.9 %collective-permute-start.1 = (bf16[4,4096]{1,0:T(4,128)(2,1)S(1)}, bf16[4,4096]{1,0:T(4,128)(2,1)S(1)}, u32[]{:S(2)}, u32[]{:S(2)}) collective-permute-start(bf16[4,4096]{1,0:T(4,128)(2,1)S(1)} %copy-done.4), channel_id=1, source_target_pairs={{0,2},{1,3},{2,0},{3,1},{4,6},{5,7},{6,4},{7,5},{8,10},{9,11},{10,... | collective-permute-start | bytes 98312 | tf_op jit(solution)/shard_map/ppermute | solution.py:236
  7.2 0.0 copy-done.1
  7.2 1.8 %shard_map.112.refs_4_ = f32[384,96]{1,0:T(8,128)S(1)} custom-call(bf16[96,4096]{1,0:T(8,128)(2,1)S(1)} %copy-done.1, bf16[4,4096]{1,0:T(4,128)(2,1)S(1)} %copy-done.4), custom_call_target="tpu_custom_call" | custom-call | flops 603979776 | bytes 786432 | tf_op jit(solution)/shard_map/pallas_call | solution.py:16
  9.1 0.0 copy-start.7
  9.1 0.0 collective-permute-done.1.other_ref
  9.1 8.8 %collective-permute-start.2 = (bf16[8,4096]{1,0:T(8,128)(2,1)S(1)}, bf16[8,4096]{1,0:T(8,128)(2,1)S(1)}, u32[]{:S(2)}, u32[]{:S(2)}) collective-permute-start(bf16[8,4096]{1,0:T(8,128)(2,1)S(1)} %shard_map.113.refs_3_.own_ref), channel_id=1, source_target_pairs={{0,1},{1,0},{2,3},{3,2},{4,5},{5,4},{6,7},{7,6},{8,9},{9,8},{10,11... | collective-permute-start | bytes 196616 | tf_op jit(solution)/shard_map/ppermute | solution.py:253
  17.9 0.0 collective-permute-done.refs_2_
  17.9 0.0 copy-done.7
  17.9 1.8 %shard_map.114 = bf16[64,2,896]{2,1,0:T(2,128)(2,1)} custom-call(s32[1]{0:T(128)S(6)} %select_n.21.side_ref.odd_ref.refs_0_, bf16[96,4096]{1,0:T(8,128)(2,1)S(1)} %copy-done.1, bf16[96,2048]{1,0:T(8,128)(2,1)S(1)} %collective-permute-done.refs_2_, bf16[8,4096]{1,0:T(8,128)(2,1)S(1)} %shard_map.113.refs_3_.own_ref, f32[384,96]{1,0:T(8,128)S(1)} %shard_map.112.refs_4_, ...), custom_call_target="tpu_custom_call" | custom-call | flops 301989888 | bytes 1572864 | tf_op jit(solution)/shard_map/pallas_call | solution.py:16
  19.7 0.0 collective-permute-done.2.other_ref
  19.8 17.2 %all-to-all-start = ((bf16[64,2,896]{2,1,0:T(2,128)(2,1)}), bf16[64,2,896]{2,1,0:T(2,128)(2,1)S(1)}, u32[]{:S(2)}, u32[]{:S(2)}) async-start(bf16[64,2,896]{2,1,0:T(2,128)(2,1)} %shard_map.114), calls=%async_computation | async-start | bytes 458752 | tf_op jit(solution)/shard_map/all_to_all | solution.py:272
  37.0 0.0 copy-start.2
  37.0 0.0 copy-start.5
  37.0 0.0 copy-start.3
  37.1 4.4 %collective-permute-start.3 = (bf16[16,4096]{1,0:T(8,128)(2,1)S(1)}, bf16[16,4096]{1,0:T(8,128)(2,1)S(1)}, u32[]{:S(2)}, u32[]{:S(2)}) collective-permute-start(bf16[16,4096]{1,0:T(8,128)(2,1)S(1)} %shard_map.116.refs_8_), channel_id=1, source_target_pairs={{0,6},{1,7},{2,4},{3,5},{4,2},{5,3},{6,0},{7,1},{8,14},{9,15},{10,... | collective-permute-start | bytes 393224 | tf_op jit(solution)/shard_map/ppermute | solution.py:271
  41.4 0.0 copy-start.8
  41.5 0.0 copy-done.2
  41.5 0.0 copy-done.5
  41.5 0.0 copy-done.3
  41.5 0.6 %copy-done.8 = s32[32]{0:T(128)S(1)} copy-done((s32[32]{0:T(128)S(1)}, s32[32]{0:T(128)}, u32[]{:S(2)}) %copy-start.8) | copy-done | bytes 152
  42.1 1.1 %shard_map.115 = (f32[32,512]{1,0:T(8,128)S(1)}, f32[32,512]{1,0:T(8,128)S(1)}, f32[256,128]{1,0:T(8,128)S(1)}) custom-call(s32[32]{0:T(128)S(1)} %copy-done.8, bf16[1,512]{1,0:T(2,128)(2,1)S(1)} %copy-done.7, bf16[32,512]{1,0:T(8,128)(2,1)S(1)} %copy-done.5, bf16[512,128]{1,0:T(8,128)(2,1)S(1)} %copy-done.2, f32[8,512]{1,0:T(8,128)S(1)} %copy-done.3), custom_call_target="tpu_custom_call" | custom-call | flops 33554432 | bytes 524288 | tf_op jit(solution)/shard_map/pallas_call | solution.py:16
  43.2 0.0 all-to-all-done.refs_2_.refs_1_
  43.2 0.9 %shard_map.118 = f32[8,8,144]{2,1,0:T(8,128)} custom-call(s32[1]{0:T(128)S(6)} %select_n.23.refs_0_, bf16[64,2,896]{2,1,0:T(2,128)(2,1)S(1)} %all-to-all-done.refs_2_.refs_1_), custom_call_target="tpu_custom_call" | custom-call | bytes 458752 | tf_op jit(solution)/shard_map/pallas_call | solution.py:16
  44.1 0.0 copy-start.6
  44.1 7.0 %all-to-all-start.1 = ((f32[8,8,144]{2,1,0:T(8,128)}), f32[8,8,144]{2,1,0:T(8,128)S(1)}, u32[]{:S(2)}, u32[]{:S(2)}) async-start(f32[8,8,144]{2,1,0:T(8,128)} %shard_map.118), calls=%async_computation.1 | async-start | bytes 131072 | tf_op jit(solution)/shard_map/all_to_all | solution.py:307
  51.1 0.0 collective-permute-done.3.refs_9_
  51.1 0.0 copy-done.6
  51.1 2.0 %shard_map.117 = (f32[8,32]{1,0:T(8,128)}, f32[8,32]{1,0:T(8,128)S(1)}, bf16[8,4096]{1,0:T(8,128)(2,1)}) custom-call(s32[32]{0:T(128)S(1)} %copy-done.8, s32[1]{0:T(128)S(6)} %select_n.20.refs_1_, bf16[64,2,896]{2,1,0:T(2,128)(2,1)S(1)} %all-to-all-done.refs_2_.refs_1_, f32[32,512]{1,0:T(8,128)S(1)} %get-tuple-element.35.refs_3_, ...), custom_call_target="tpu_custom_call" | custom-call | flops 2097152 | bytes 524288 | tf_op jit(solution)/shard_map/pallas_call | solution.py:16
  53.1 0.2 all-to-all-done.1.refs_3_
  53.3 0.7 %shard_map.119 = (f32[4,144]{1,0:T(4,128)}, f32[8,144]{1,0:T(8,128)}) custom-call(s32[1]{0:T(128)S(6)} %select_n.22.core_ref.refs_0_, s32[1]{0:T(128)S(6)} %select_n.20.refs_1_, f32[8,32]{1,0:T(8,128)S(1)} %get-tuple-element.41.refs_2_, f32[8,8,144]{2,1,0:T(8,128)S(1)} %all-to-all-done.1.refs_3_), custom_call_target="tpu_custom_call" | custom-call | bytes 32768 | tf_op jit(solution)/shard_map/pallas_call | solution.py:16
  (3 shorter events, 0.1 us)
Async XLA Ops:
  0.7 1.1 %copy-start = (bf16[96,4096]{1,0:T(8,128)(2,1)S(1)}, bf16[96,4096]{1,0:T(8,128)(2,1)}, u32[]{:S(2)}) copy-start(bf16[96,4096]{1,0:T(8,128)(2,1)} %refs_1_.3) | copy-start | bytes 2359300
  1.8 1.5 %copy-start.4 = (bf16[4,4096]{1,0:T(4,128)(2,1)S(1)}, bf16[4,4096]{1,0:T(4,128)(2,1)}, u32[]{:S(2)}) copy-start(bf16[4,4096]{1,0:T(4,128)(2,1)} %own_ref.1) | copy-start | bytes 98308
  1.8 5.4 %copy-start.1 = (bf16[96,4096]{1,0:T(8,128)(2,1)S(1)}, bf16[96,4096]{1,0:T(8,128)(2,1)}, u32[]{:S(2)}) copy-start(bf16[96,4096]{1,0:T(8,128)(2,1)} %refs_1_.3) | copy-start | bytes 2359300
  1.8 16.1 %collective-permute-start = (bf16[96,2048]{1,0:T(8,128)(2,1)S(1)}, bf16[96,2048]{1,0:T(8,128)(2,1)S(1)}, u32[]{:S(2)}, u32[]{:S(2)}) collective-permute-start(bf16[96,2048]{1,0:T(8,128)(2,1)S(1)} %shard_map.111), channel_id=1, source_target_pairs={{8,0},{16,8},{24,16},{32,24},{40,32},{48,40},{56,48},{64,56},{72,6... | collective-permute-start | bytes 1179656 | tf_op jit(solution)/shard_map/ppermute | solution.py:235
  3.3 5.8 %collective-permute-start.1 = (bf16[4,4096]{1,0:T(4,128)(2,1)S(1)}, bf16[4,4096]{1,0:T(4,128)(2,1)S(1)}, u32[]{:S(2)}, u32[]{:S(2)}) collective-permute-start(bf16[4,4096]{1,0:T(4,128)(2,1)S(1)} %copy-done.4), channel_id=1, source_target_pairs={{0,2},{1,3},{2,0},{3,1},{4,6},{5,7},{6,4},{7,5},{8,10},{9,11},{10,... | collective-permute-start | bytes 98312 | tf_op jit(solution)/shard_map/ppermute | solution.py:236
  9.1 8.8 %copy-start.7 = (bf16[1,512]{1,0:T(2,128)(2,1)S(1)}, bf16[1,512]{1,0:T(2,128)(2,1)}, u32[]{:S(2)}) copy-start(bf16[1,512]{1,0:T(2,128)(2,1)} %x_ref.1) | copy-start | bytes 3076
  9.1 10.6 %collective-permute-start.2 = (bf16[8,4096]{1,0:T(8,128)(2,1)S(1)}, bf16[8,4096]{1,0:T(8,128)(2,1)S(1)}, u32[]{:S(2)}, u32[]{:S(2)}) collective-permute-start(bf16[8,4096]{1,0:T(8,128)(2,1)S(1)} %shard_map.113.refs_3_.own_ref), channel_id=1, source_target_pairs={{0,1},{1,0},{2,3},{3,2},{4,5},{5,4},{6,7},{7,6},{8,9},{9,8},{10,11... | collective-permute-start | bytes 196616 | tf_op jit(solution)/shard_map/ppermute | solution.py:253
  19.8 23.4 %all-to-all-start = ((bf16[64,2,896]{2,1,0:T(2,128)(2,1)}), bf16[64,2,896]{2,1,0:T(2,128)(2,1)S(1)}, u32[]{:S(2)}, u32[]{:S(2)}) async-start(bf16[64,2,896]{2,1,0:T(2,128)(2,1)} %shard_map.114), calls=%async_computation | async-start | bytes 458752 | tf_op jit(solution)/shard_map/all_to_all | solution.py:272
  37.0 4.5 %copy-start.2 = (bf16[512,128]{1,0:T(8,128)(2,1)S(1)}, bf16[512,128]{1,0:T(8,128)(2,1)}, u32[]{:S(2)}) copy-start(bf16[512,128]{1,0:T(8,128)(2,1)} %z_ref.1) | copy-start | bytes 393220
  37.0 4.5 %copy-start.5 = (bf16[32,512]{1,0:T(8,128)(2,1)S(1)}, bf16[32,512]{1,0:T(8,128)(2,1)}, u32[]{:S(2)}) copy-start(bf16[32,512]{1,0:T(8,128)(2,1)} %y_ref.1) | copy-start | bytes 98308
  37.0 4.4 %copy-start.3 = (f32[8,512]{1,0:T(8,128)S(1)}, f32[8,512]{1,0:T(8,128)}, u32[]{:S(2)}) copy-start(f32[8,512]{1,0:T(8,128)} %refs_6_.1) | copy-start | bytes 49156
  37.1 14.1 %collective-permute-start.3 = (bf16[16,4096]{1,0:T(8,128)(2,1)S(1)}, bf16[16,4096]{1,0:T(8,128)(2,1)S(1)}, u32[]{:S(2)}, u32[]{:S(2)}) collective-permute-start(bf16[16,4096]{1,0:T(8,128)(2,1)S(1)} %shard_map.116.refs_8_), channel_id=1, source_target_pairs={{0,6},{1,7},{2,4},{3,5},{4,2},{5,3},{6,0},{7,1},{8,14},{9,15},{10,... | collective-permute-start | bytes 393224 | tf_op jit(solution)/shard_map/ppermute | solution.py:271
  41.4 0.7 %copy-start.8 = (s32[32]{0:T(128)S(1)}, s32[32]{0:T(128)}, u32[]{:S(2)}) copy-start(s32[32]{0:T(128)} %refs_0_.3) | copy-start | bytes 388
  44.1 7.0 %copy-start.6 = (f32[32,32]{1,0:T(8,128)S(1)}, f32[32,32]{1,0:T(8,128)}, u32[]{:S(2)}) copy-start(f32[32,32]{1,0:T(8,128)} %refs_7_.1) | copy-start | bytes 12292
  44.1 9.2 %all-to-all-start.1 = ((f32[8,8,144]{2,1,0:T(8,128)}), f32[8,8,144]{2,1,0:T(8,128)S(1)}, u32[]{:S(2)}, u32[]{:S(2)}) async-start(f32[8,8,144]{2,1,0:T(8,128)} %shard_map.118), calls=%async_computation.1 | async-start | bytes 131072 | tf_op jit(solution)/shard_map/all_to_all | solution.py:307

commit v2 on v1

--- a/solution.py
+++ b/solution.py
@@ -64,7 +64,8 @@
     out_ref[...] = basis_ref[...]
 
 
-def outer_gram(ranks, side_ref, basis_ref, following_ref, eim_ref, inner_ref, x_ref, out_ref):
+def outer_gram(ranks, side_ref, basis_ref, following_ref, eim_ref, inner_ref, x_ref, y_ref, z_ref, out_ref):
+    del y_ref, z_ref
     half = following_ref.shape[1]
     depth = inner_ref.shape[0] // 2
     total = []
@@ -255,20 +256,12 @@
     packed = call(
         lambda *refs: outer_gram(ranks, *refs),
         shape((slabs, 2, terms * rank + modes), BF16),
-        (side, basis, near, eim_pair, inner, x_modes),
-        specs=[SMEM] + [VMEM] * 5,
+        (side, basis, near, eim_pair, inner, x_modes, y_modes, z_modes),
+        specs=[SMEM] + [VMEM] * 7,
         flops=gram_flops,
         moved=4 * basis.size,
     )
     packed, eim_other, factors = lax.optimization_barrier((packed, eim_other, coefficients))
-    eim_near = call(
-        two_cores,
-        shape((4 * terms, cells), BF16),
-        (core, eim_pair, eim_other),
-        specs=[SMEM, VMEM, VMEM],
-        moved=16 * eim_basis.size,
-    )
-    eim_far = lax.ppermute(eim_near, term, [(i, i ^ (groups - 2)) for i in range(groups)])
     arrived = lax.all_to_all(packed, space, 0, 0, axis_index_groups=[ranks], tiled=True)
     at_y, at_z, conductivity = call(
         field,
@@ -283,6 +276,17 @@
         flops=2 * snaps * width_y * modes * width_z,
         moved=4 * points * cells,
     )
+    eim_other, at_y, at_z, conductivity = lax.optimization_barrier(
+        (eim_other, at_y, at_z, conductivity)
+    )
+    eim_near = call(
+        two_cores,
+        shape((4 * terms, cells), BF16),
+        (core, eim_pair, eim_other),
+        specs=[SMEM, VMEM, VMEM],
+        moved=16 * eim_basis.size,
+    )
+    eim_far = lax.ppermute(eim_near, term, [(i, i ^ (groups - 2)) for i in range(groups)])
     arrived, at_y, at_z, conductivity = lax.optimization_barrier(
         (arrived, at_y, at_z, conductivity)
     )

time: 54.5 us -> 54.7 us (level)
  no operation moved by 1% of the time
where the time goes in v2:
time: 54.7 us; the launch traced here: 54.2 us
  starting transfers between devices  42.8 us (78%)
  Pallas kernels  8.53 us (16%)
  local copies, waits for them, and re-layouts  1.8 us (3%)
  between operations  0.87 us (2%)
    all_to_all x1, starting transfers between devices, local(): lax.all_to_all(packed, space, 0, 0, axis_index_groups=[ranks], tiled=True)  17.3 us
    ppermute x1, starting transfers between devices, local(): eim_other = lax.ppermute(eim_pair, term, swap)  8.73 us
    pallas_call x8, Pallas kernels, call(): pl.pallas_call(body, out_shape=out_shape, in_specs=specs or [VMEM] * len(...  8.5 us
    all_to_all x1, starting transfers between devices, local(): lax.all_to_all(spread, term, 0, 0, axis_index_groups=[term_ranks], tiled=...  6.96 us
    ppermute x1, starting transfers between devices, local(): lax.ppermute(eim_near, term, [(i, i ^ groups - 2) for i in range(groups)])  4.39 us
    ppermute x1, starting transfers between devices, local(): lax.ppermute(eim_basis, term, [(i, i ^ 2) for i in range(groups)])  3.95 us
    unnamed x18, local copies, waits for them, and re-layouts  1.8 us
    ppermute x1, starting transfers between devices, local(): near = lax.ppermute(mine, space, [(i + 1, i) for i in range(slabs - 1)])  1.42 us
  transfers between devices with their start and end apart: 6, of which 1 were waited for; matrix products, arithmetic and copies ran while one was open for 0% of the time, Pallas kernels for 14%

profile of v2, /device:TPU:1, one launch (start us, length us, event | category | flops | bytes accessed | tf_op | source)
XLA Modules:
  0.0 54.2 jit_solution(6888098198075688916)
XLA Ops:
  0.7 0.0 copy-start
  0.7 1.1 %copy-done = bf16[96,4096]{1,0:T(8,128)(2,1)S(1)} copy-done((bf16[96,4096]{1,0:T(8,128)(2,1)S(1)}, bf16[96,4096]{1,0:T(8,128)(2,1)}, u32[]{:S(2)}) %copy-start) | copy-done | bytes 786456
  1.8 0.0 copy-start.5
  1.8 0.0 copy-start.1
  1.8 1.4 %collective-permute-start = (bf16[96,2048]{1,0:T(8,128)(2,1)S(1)}, bf16[96,2048]{1,0:T(8,128)(2,1)S(1)}, u32[]{:S(2)}, u32[]{:S(2)}) collective-permute-start(bf16[96,2048]{1,0:T(8,128)(2,1)S(1)} %shard_map.111), channel_id=1, source_target_pairs={{8,0},{16,8},{24,16},{32,24},{40,32},{48,40},{56,48},{64,56},{72,6... | collective-permute-start | bytes 1179656 | tf_op jit(solution)/shard_map/ppermute | solution.py:236
  3.3 0.0 copy-done.5
  3.3 3.9 %collective-permute-start.1 = (bf16[4,4096]{1,0:T(4,128)(2,1)S(1)}, bf16[4,4096]{1,0:T(4,128)(2,1)S(1)}, u32[]{:S(2)}, u32[]{:S(2)}) collective-permute-start(bf16[4,4096]{1,0:T(4,128)(2,1)S(1)} %copy-done.5), channel_id=1, source_target_pairs={{0,2},{1,3},{2,0},{3,1},{4,6},{5,7},{6,4},{7,5},{8,10},{9,11},{10,... | collective-permute-start | bytes 98312 | tf_op jit(solution)/shard_map/ppermute | solution.py:237
  7.2 0.0 copy-done.1
  7.2 0.0 copy-start.3
  7.2 0.0 copy-start.7
  7.3 1.8 %shard_map.112.refs_4_ = f32[384,96]{1,0:T(8,128)S(1)} custom-call(bf16[96,4096]{1,0:T(8,128)(2,1)S(1)} %copy-done.1, bf16[4,4096]{1,0:T(4,128)(2,1)S(1)} %copy-done.5), custom_call_target="tpu_custom_call" | custom-call | flops 603979776 | bytes 786432 | tf_op jit(solution)/shard_map/pallas_call | solution.py:16
  9.1 0.0 copy-start.2
  9.1 0.0 collective-permute-done.1.other_ref
  9.2 8.7 %collective-permute-start.2 = (bf16[8,4096]{1,0:T(8,128)(2,1)S(1)}, bf16[8,4096]{1,0:T(8,128)(2,1)S(1)}, u32[]{:S(2)}, u32[]{:S(2)}) collective-permute-start(bf16[8,4096]{1,0:T(8,128)(2,1)S(1)} %shard_map.113.refs_3_.own_ref), channel_id=1, source_target_pairs={{0,1},{1,0},{2,3},{3,2},{4,5},{5,4},{6,7},{7,6},{8,9},{9,8},{10,11... | collective-permute-start | bytes 196616 | tf_op jit(solution)/shard_map/ppermute | solution.py:254
  17.9 0.0 collective-permute-done.refs_2_
  17.9 0.0 copy-done.3
  17.9 0.0 copy-done.7
  17.9 0.0 copy-done.2
  17.9 1.8 %shard_map.114 = bf16[64,2,896]{2,1,0:T(2,128)(2,1)} custom-call(s32[1]{0:T(128)S(6)} %select_n.21.side_ref.odd_ref.refs_0_, bf16[96,4096]{1,0:T(8,128)(2,1)S(1)} %copy-done.1, bf16[96,2048]{1,0:T(8,128)(2,1)S(1)} %collective-permute-done.refs_2_, bf16[8,4096]{1,0:T(8,128)(2,1)S(1)} %shard_map.113.refs_3_.own_ref, f32[384,96]{1,0:T(8,128)S(1)} %shard_map.112.refs_4_, ...), custom_call_target="tpu_custom_call" | custom-call | flops 301989888 | bytes 1572864 | tf_op jit(solution)/shard_map/pallas_call | solution.py:16
  19.8 0.0 collective-permute-done.2.other_ref
  19.8 0.0 copy-start.4
  19.8 17.3 %all-to-all-start = ((bf16[64,2,896]{2,1,0:T(2,128)(2,1)}), bf16[64,2,896]{2,1,0:T(2,128)(2,1)S(1)}, u32[]{:S(2)}, u32[]{:S(2)}) async-start(bf16[64,2,896]{2,1,0:T(2,128)(2,1)} %shard_map.114), calls=%async_computation | async-start | bytes 458752 | tf_op jit(solution)/shard_map/all_to_all | solution.py:265
  37.1 0.0 copy-start.8
  37.1 0.0 copy-done.4
  37.1 0.6 %copy-done.8 = s32[32]{0:T(128)S(1)} copy-done((s32[32]{0:T(128)S(1)}, s32[32]{0:T(128)}, u32[]{:S(2)}) %copy-start.8) | copy-done | bytes 152
  37.8 1.1 %shard_map.115 = (f32[32,512]{1,0:T(8,128)S(1)}, f32[32,512]{1,0:T(8,128)S(1)}, f32[256,128]{1,0:T(8,128)S(1)}) custom-call(s32[32]{0:T(128)S(1)} %copy-done.8, bf16[1,512]{1,0:T(2,128)(2,1)S(1)} %copy-done.7, bf16[32,512]{1,0:T(8,128)(2,1)S(1)} %copy-done.3, bf16[512,128]{1,0:T(8,128)(2,1)S(1)} %copy-done.2, f32[8,512]{1,0:T(8,128)S(1)} %copy-done.4), custom_call_target="tpu_custom_call" | custom-call | flops 33554432 | bytes 524288 | tf_op jit(solution)/shard_map/pallas_call | solution.py:16
  38.9 4.4 %collective-permute-start.3 = (bf16[16,4096]{1,0:T(8,128)(2,1)S(1)}, bf16[16,4096]{1,0:T(8,128)(2,1)S(1)}, u32[]{:S(2)}, u32[]{:S(2)}) collective-permute-start(bf16[16,4096]{1,0:T(8,128)(2,1)S(1)} %shard_map.116.refs_8_), channel_id=1, source_target_pairs={{0,6},{1,7},{2,4},{3,5},{4,2},{5,3},{6,0},{7,1},{8,14},{9,15},{10,... | collective-permute-start | bytes 393224 | tf_op jit(solution)/shard_map/ppermute | solution.py:289
  43.3 0.0 all-to-all-done.refs_2_.refs_1_
  43.3 0.9 %shard_map.118 = f32[8,8,144]{2,1,0:T(8,128)} custom-call(s32[1]{0:T(128)S(6)} %select_n.23.refs_0_, bf16[64,2,896]{2,1,0:T(2,128)(2,1)S(1)} %all-to-all-done.refs_2_.refs_1_), custom_call_target="tpu_custom_call" | custom-call | bytes 458752 | tf_op jit(solution)/shard_map/pallas_call | solution.py:16
  44.2 0.0 copy-start.6
  44.2 7.0 %all-to-all-start.1 = ((f32[8,8,144]{2,1,0:T(8,128)}), f32[8,8,144]{2,1,0:T(8,128)S(1)}, u32[]{:S(2)}, u32[]{:S(2)}) async-start(f32[8,8,144]{2,1,0:T(8,128)} %shard_map.118), calls=%async_computation.1 | async-start | bytes 131072 | tf_op jit(solution)/shard_map/all_to_all | solution.py:311
  51.2 0.0 collective-permute-done.3.refs_9_
  51.2 0.0 copy-done.6
  51.2 2.0 %shard_map.117 = (f32[8,32]{1,0:T(8,128)}, f32[8,32]{1,0:T(8,128)S(1)}, bf16[8,4096]{1,0:T(8,128)(2,1)}) custom-call(s32[32]{0:T(128)S(1)} %copy-done.8, s32[1]{0:T(128)S(6)} %select_n.20.refs_1_, bf16[64,2,896]{2,1,0:T(2,128)(2,1)S(1)} %all-to-all-done.refs_2_.refs_1_, f32[32,512]{1,0:T(8,128)S(1)} %get-tuple-element.43.refs_3_, ...), custom_call_target="tpu_custom_call" | custom-call | flops 2097152 | bytes 524288 | tf_op jit(solution)/shard_map/pallas_call | solution.py:16
  53.3 0.2 all-to-all-done.1.refs_3_
  53.4 0.7 %shard_map.119 = (f32[4,144]{1,0:T(4,128)}, f32[8,144]{1,0:T(8,128)}) custom-call(s32[1]{0:T(128)S(6)} %select_n.22.core_ref.refs_0_, s32[1]{0:T(128)S(6)} %select_n.20.refs_1_, f32[8,32]{1,0:T(8,128)S(1)} %get-tuple-element.49.refs_2_, f32[8,8,144]{2,1,0:T(8,128)S(1)} %all-to-all-done.1.refs_3_), custom_call_target="tpu_custom_call" | custom-call | bytes 32768 | tf_op jit(solution)/shard_map/pallas_call | solution.py:16
  (3 shorter events, 0.1 us)
Async XLA Ops:
  0.7 1.1 %copy-start = (bf16[96,4096]{1,0:T(8,128)(2,1)S(1)}, bf16[96,4096]{1,0:T(8,128)(2,1)}, u32[]{:S(2)}) copy-start(bf16[96,4096]{1,0:T(8,128)(2,1)} %refs_1_.3) | copy-start | bytes 2359300
  1.8 1.5 %copy-start.5 = (bf16[4,4096]{1,0:T(4,128)(2,1)S(1)}, bf16[4,4096]{1,0:T(4,128)(2,1)}, u32[]{:S(2)}) copy-start(bf16[4,4096]{1,0:T(4,128)(2,1)} %own_ref.1) | copy-start | bytes 98308
  1.8 5.4 %copy-start.1 = (bf16[96,4096]{1,0:T(8,128)(2,1)S(1)}, bf16[96,4096]{1,0:T(8,128)(2,1)}, u32[]{:S(2)}) copy-start(bf16[96,4096]{1,0:T(8,128)(2,1)} %refs_1_.3) | copy-start | bytes 2359300
  1.8 16.1 %collective-permute-start = (bf16[96,2048]{1,0:T(8,128)(2,1)S(1)}, bf16[96,2048]{1,0:T(8,128)(2,1)S(1)}, u32[]{:S(2)}, u32[]{:S(2)}) collective-permute-start(bf16[96,2048]{1,0:T(8,128)(2,1)S(1)} %shard_map.111), channel_id=1, source_target_pairs={{8,0},{16,8},{24,16},{32,24},{40,32},{48,40},{56,48},{64,56},{72,6... | collective-permute-start | bytes 1179656 | tf_op jit(solution)/shard_map/ppermute | solution.py:236
  3.3 5.9 %collective-permute-start.1 = (bf16[4,4096]{1,0:T(4,128)(2,1)S(1)}, bf16[4,4096]{1,0:T(4,128)(2,1)S(1)}, u32[]{:S(2)}, u32[]{:S(2)}) collective-permute-start(bf16[4,4096]{1,0:T(4,128)(2,1)S(1)} %copy-done.5), channel_id=1, source_target_pairs={{0,2},{1,3},{2,0},{3,1},{4,6},{5,7},{6,4},{7,5},{8,10},{9,11},{10,... | collective-permute-start | bytes 98312 | tf_op jit(solution)/shard_map/ppermute | solution.py:237
  7.2 10.7 %copy-start.3 = (bf16[32,512]{1,0:T(8,128)(2,1)S(1)}, bf16[32,512]{1,0:T(8,128)(2,1)}, u32[]{:S(2)}) copy-start(bf16[32,512]{1,0:T(8,128)(2,1)} %y_ref.1) | copy-start | bytes 98308
  7.2 10.7 %copy-start.7 = (bf16[1,512]{1,0:T(2,128)(2,1)S(1)}, bf16[1,512]{1,0:T(2,128)(2,1)}, u32[]{:S(2)}) copy-start(bf16[1,512]{1,0:T(2,128)(2,1)} %x_ref.1) | copy-start | bytes 3076
  9.1 8.8 %copy-start.2 = (bf16[512,128]{1,0:T(8,128)(2,1)S(1)}, bf16[512,128]{1,0:T(8,128)(2,1)}, u32[]{:S(2)}) copy-start(bf16[512,128]{1,0:T(8,128)(2,1)} %z_ref.1) | copy-start | bytes 393220
  9.2 10.6 %collective-permute-start.2 = (bf16[8,4096]{1,0:T(8,128)(2,1)S(1)}, bf16[8,4096]{1,0:T(8,128)(2,1)S(1)}, u32[]{:S(2)}, u32[]{:S(2)}) collective-permute-start(bf16[8,4096]{1,0:T(8,128)(2,1)S(1)} %shard_map.113.refs_3_.own_ref), channel_id=1, source_target_pairs={{0,1},{1,0},{2,3},{3,2},{4,5},{5,4},{6,7},{7,6},{8,9},{9,8},{10,11... | collective-permute-start | bytes 196616 | tf_op jit(solution)/shard_map/ppermute | solution.py:254
  19.8 17.3 %copy-start.4 = (f32[8,512]{1,0:T(8,128)S(1)}, f32[8,512]{1,0:T(8,128)}, u32[]{:S(2)}) copy-start(f32[8,512]{1,0:T(8,128)} %refs_6_.3) | copy-start | bytes 49156
  19.8 23.5 %all-to-all-start = ((bf16[64,2,896]{2,1,0:T(2,128)(2,1)}), bf16[64,2,896]{2,1,0:T(2,128)(2,1)S(1)}, u32[]{:S(2)}, u32[]{:S(2)}) async-start(bf16[64,2,896]{2,1,0:T(2,128)(2,1)} %shard_map.114), calls=%async_computation | async-start | bytes 458752 | tf_op jit(solution)/shard_map/all_to_all | solution.py:265
  37.1 0.7 %copy-start.8 = (s32[32]{0:T(128)S(1)}, s32[32]{0:T(128)}, u32[]{:S(2)}) copy-start(s32[32]{0:T(128)} %refs_0_.3) | copy-start | bytes 388
  38.9 12.3 %collective-permute-start.3 = (bf16[16,4096]{1,0:T(8,128)(2,1)S(1)}, bf16[16,4096]{1,0:T(8,128)(2,1)S(1)}, u32[]{:S(2)}, u32[]{:S(2)}) collective-permute-start(bf16[16,4096]{1,0:T(8,128)(2,1)S(1)} %shard_map.116.refs_8_), channel_id=1, source_target_pairs={{0,6},{1,7},{2,4},{3,5},{4,2},{5,3},{6,0},{7,1},{8,14},{9,15},{10,... | collective-permute-start | bytes 393224 | tf_op jit(solution)/shard_map/ppermute | solution.py:289
  44.2 7.0 %copy-start.6 = (f32[32,32]{1,0:T(8,128)S(1)}, f32[32,32]{1,0:T(8,128)}, u32[]{:S(2)}) copy-start(f32[32,32]{1,0:T(8,128)} %refs_7_.3) | copy-start | bytes 12292
  44.2 9.2 %all-to-all-start.1 = ((f32[8,8,144]{2,1,0:T(8,128)}), f32[8,8,144]{2,1,0:T(8,128)S(1)}, u32[]{:S(2)}, u32[]{:S(2)}) async-start(f32[8,8,144]{2,1,0:T(8,128)} %shard_map.118), calls=%async_computation.1 | async-start | bytes 131072 | tf_op jit(solution)/shard_map/all_to_all | solution.py:311

commit v3 on v1

--- a/solution.py
+++ b/solution.py
@@ -97,15 +97,6 @@
     even = odd_ref[0] == 0
     first, second = jnp.where(even, own, other), jnp.where(even, other, own)
     out_ref[...] = jnp.concatenate([first, second], 0).astype(BF16)
-
-
-def two_cores(core_ref, own_ref, other_ref, out_ref):
-    own, other = own_ref[...].astype(F32), other_ref[...].astype(F32)
-    even = core_ref[0] == 0
-    first, second = jnp.where(even, own, other), jnp.where(even, other, own)
-    terms = own.shape[0] // 2
-    rows = [first[:terms], second[:terms], first[terms:], second[terms:]]
-    out_ref[...] = jnp.concatenate(rows, 0).astype(BF16)
 
 
 def field(
@@ -185,19 +176,18 @@
 
 def assembly(turn, core_ref, chip_ref, turned_ref, operators_ref, own_ref, out_ref):
     turned = turned_ref[...]
-    count, both = operators_ref.shape[:2]
-    terms = both // 2
+    count, terms = operators_ref.shape[:2]
     total = jnp.zeros(out_ref.shape, F32)
-    for first in (0, 1, 4, 5):
-        at = (first + count - turn) % count
-        block = operators_ref[at] + operators_ref[at + 2]
-        for j in range(both):
-            q = (first + 2 * (j // terms)) * terms + j % terms
+    for chip in range(count // 2):
+        at = (2 * chip + count - turn) % count
+        block = operators_ref[at] + operators_ref[at + 1]
+        for j in range(terms):
+            q = chip * terms + j
             total += turned[:, q : q + 1] * block[j : j + 1]
     out_ref[...] = total
-    at = (4 * (chip_ref[0] // 2) + core_ref[0] + count - turn) % count
-    own = operators_ref[at] + operators_ref[at + 2]
-    own_ref[...] = jnp.where(chip_ref[0] % 2 == 0, own[:terms], own[terms:])
+    at = (2 * chip_ref[0] + count - turn) % count
+    own = operators_ref[at] + operators_ref[at + 1]
+    own_ref[...] = jnp.where(core_ref[0] == 0, own[: terms // 2], own[terms // 2 :])
 
 
 def local(x_modes, y_modes, z_modes, coefficients, magic_cells, interp_inverse, eim_basis, basis):
@@ -231,9 +221,9 @@
         ),
         compiler_params=pltpu.CompilerParams(vmem_limit_bytes=32 << 20),
         cost_estimate=pl.CostEstimate(flops=0, bytes_accessed=2 * basis.size, transcendentals=0),
-    )(side, basis)
+    )(core, basis)
     near = lax.ppermute(mine, space, [(i + 1, i) for i in range(slabs - 1)])
-    eim_beside = lax.ppermute(eim_basis, term, [(i, i ^ 2) for i in range(groups)])
+    eim_other = lax.ppermute(eim_basis, term, swap)
     gram_flops = 2 * rank * rank * terms * cells
     inner = call(
         lambda *refs: inner_gram(width_z, *refs),
@@ -242,29 +232,29 @@
         flops=2 * gram_flops,
         moved=2 * basis.size,
     )
-    eim_beside, inner = lax.optimization_barrier((eim_beside, inner))
+    eim_other, inner = lax.optimization_barrier((eim_other, inner))
     eim_pair = call(
         in_order,
         shape((2 * terms, cells), BF16),
-        (side, eim_basis, eim_beside),
+        (core, eim_basis, eim_other),
         specs=[SMEM, VMEM, VMEM],
         moved=8 * eim_basis.size,
     )
-    eim_other = lax.ppermute(eim_pair, term, swap)
+    eim_beside = lax.ppermute(eim_pair, term, [(i, i ^ 2) for i in range(groups)])
     near, inner, eim_pair = lax.optimization_barrier((near, inner, eim_pair))
     packed = call(
         lambda *refs: outer_gram(ranks, *refs),
         shape((slabs, 2, terms * rank + modes), BF16),
-        (side, basis, near, eim_pair, inner, x_modes),
+        (core, basis, near, eim_pair, inner, x_modes),
         specs=[SMEM] + [VMEM] * 5,
         flops=gram_flops,
         moved=4 * basis.size,
     )
-    packed, eim_other, factors = lax.optimization_barrier((packed, eim_other, coefficients))
+    packed, eim_beside, factors = lax.optimization_barrier((packed, eim_beside, coefficients))
     eim_near = call(
-        two_cores,
+        in_order,
         shape((4 * terms, cells), BF16),
-        (core, eim_pair, eim_other),
+        (side, eim_pair, eim_beside),
         specs=[SMEM, VMEM, VMEM],
         moved=16 * eim_basis.size,
     )

time: 54.5 us -> 54.6 us (level)
  waiting for transfers between devices: 0.2 us -> 2.03 us
  starting transfers between devices: 42.7 us -> 41 us
    ppermute x2, starting transfers between devices: 12.7 us -> 10.7 us  [the longest x1 8.79 us: local(): eim_other = lax.ppermute(eim_basis, term, swap)]
    ppermute x2, waiting for transfers between devices: 0.01 us -> 1.84 us  [the longest x1 1.83 us: local(): lax.ppermute(eim_pair, term, [(i, i ^ 2) for i in range(groups)])]
  transfers between devices with their start and end apart: 6 -> 6, of which waited for: 1 -> 2; matrix products, arithmetic and copies ran while one was open for 0% -> 0% of each run, Pallas kernels for 14% -> 14%
where the time goes in v3:
time: 54.6 us; the launch traced here: 54.2 us
  starting transfers between devices  41 us (75%)
  Pallas kernels  8.52 us (16%)
  waiting for transfers between devices  2.03 us (4%)
  local copies, waits for them, and re-layouts  1.78 us (3%)
  between operations  0.88 us (2%)
    all_to_all x1, starting transfers between devices, local(): lax.all_to_all(packed, space, 0, 0, axis_index_groups=[ranks], tiled=True)  17.4 us
    ppermute x1, starting transfers between devices, local(): eim_other = lax.ppermute(eim_basis, term, swap)  8.79 us
    pallas_call x8, Pallas kernels, call(): pl.pallas_call(body, out_shape=out_shape, in_specs=specs or [VMEM] * len(...  8.49 us
    all_to_all x1, starting transfers between devices, local(): lax.all_to_all(spread, term, 0, 0, axis_index_groups=[term_ranks], tiled=...  6.97 us
    ppermute x1, starting transfers between devices, local(): lax.ppermute(eim_near, term, [(i, i ^ groups - 2) for i in range(groups)])  4.51 us
    ppermute x1, starting transfers between devices, local(): lax.ppermute(eim_pair, term, [(i, i ^ 2) for i in range(groups)])  1.92 us
    ppermute x1, waiting for transfers between devices, local(): lax.ppermute(eim_pair, term, [(i, i ^ 2) for i in range(groups)])  1.83 us
    unnamed x18, local copies, waits for them, and re-layouts  1.78 us
  transfers between devices with their start and end apart: 6, of which 2 were waited for; matrix products, arithmetic and copies ran while one was open for 0% of the time, Pallas kernels for 14%

profile of v3, /device:TPU:1, one launch (start us, length us, event | category | flops | bytes accessed | tf_op | source)
XLA Modules:
  0.0 54.2 jit_solution(956139218249645440)
XLA Ops:
  0.6 0.0 copy-start
  0.7 1.1 %copy-done = bf16[96,4096]{1,0:T(8,128)(2,1)S(1)} copy-done((bf16[96,4096]{1,0:T(8,128)(2,1)S(1)}, bf16[96,4096]{1,0:T(8,128)(2,1)}, u32[]{:S(2)}) %copy-start) | copy-done | bytes 786456
  1.8 0.0 copy-start.4
  1.8 0.0 copy-start.1
  1.8 1.4 %collective-permute-start = (bf16[96,2048]{1,0:T(8,128)(2,1)S(1)}, bf16[96,2048]{1,0:T(8,128)(2,1)S(1)}, u32[]{:S(2)}, u32[]{:S(2)}) collective-permute-start(bf16[96,2048]{1,0:T(8,128)(2,1)S(1)} %shard_map.111), channel_id=1, source_target_pairs={{8,0},{16,8},{24,16},{32,24},{40,32},{48,40},{56,48},{64,56},{72,6... | collective-permute-start | bytes 1179656 | tf_op jit(solution)/shard_map/ppermute | solution.py:225
  3.2 0.0 copy-done.4
  3.3 8.8 %collective-permute-start.1 = (bf16[4,4096]{1,0:T(4,128)(2,1)S(1)}, bf16[4,4096]{1,0:T(4,128)(2,1)S(1)}, u32[]{:S(2)}, u32[]{:S(2)}) collective-permute-start(bf16[4,4096]{1,0:T(4,128)(2,1)S(1)} %copy-done.4), channel_id=1, source_target_pairs={{0,1},{1,0},{2,3},{3,2},{4,5},{5,4},{6,7},{7,6},{8,9},{9,8},{10,11... | collective-permute-start | bytes 98312 | tf_op jit(solution)/shard_map/ppermute | solution.py:226
  12.0 0.0 copy-done.1
  12.1 1.8 %shard_map.112.refs_4_ = f32[384,96]{1,0:T(8,128)S(1)} custom-call(bf16[96,4096]{1,0:T(8,128)(2,1)S(1)} %copy-done.1, bf16[4,4096]{1,0:T(4,128)(2,1)S(1)} %copy-done.4), custom_call_target="tpu_custom_call" | custom-call | flops 603979776 | bytes 786432 | tf_op jit(solution)/shard_map/pallas_call | solution.py:16
  13.9 0.0 copy-start.7
  13.9 0.0 collective-permute-done.1.other_ref
  14.0 1.9 %collective-permute-start.2 = (bf16[8,4096]{1,0:T(8,128)(2,1)S(1)}, bf16[8,4096]{1,0:T(8,128)(2,1)S(1)}, u32[]{:S(2)}, u32[]{:S(2)}) collective-permute-start(bf16[8,4096]{1,0:T(8,128)(2,1)S(1)} %shard_map.113.refs_3_.own_ref), channel_id=1, source_target_pairs={{0,2},{1,3},{2,0},{3,1},{4,6},{5,7},{6,4},{7,5},{8,10},{9,11},{10,... | collective-permute-start | bytes 196616 | tf_op jit(solution)/shard_map/ppermute | solution.py:243
  15.9 0.0 collective-permute-done.refs_2_
  15.9 0.0 copy-done.7
  15.9 1.8 %shard_map.114 = bf16[64,2,896]{2,1,0:T(2,128)(2,1)} custom-call(s32[1]{0:T(128)S(6)} %select_n.21.side_ref.odd_ref.refs_0_, bf16[96,4096]{1,0:T(8,128)(2,1)S(1)} %copy-done.1, bf16[96,2048]{1,0:T(8,128)(2,1)S(1)} %collective-permute-done.refs_2_, bf16[8,4096]{1,0:T(8,128)(2,1)S(1)} %shard_map.113.refs_3_.own_ref, f32[384,96]{1,0:T(8,128)S(1)} %shard_map.112.refs_4_, ...), custom_call_target="tpu_custom_call" | custom-call | flops 301989888 | bytes 1572864 | tf_op jit(solution)/shard_map/pallas_call | solution.py:16
  17.7 1.8 %collective-permute-done.2.other_ref = bf16[8,4096]{1,0:T(8,128)(2,1)S(1)} collective-permute-done((bf16[8,4096]{1,0:T(8,128)(2,1)S(1)}, bf16[8,4096]{1,0:T(8,128)(2,1)S(1)}, u32[]{:S(2)}, u32[]{:S(2)}) %collective-permute-start.2) | collective-permute-done | bytes 65568 | tf_op jit(solution)/shard_map/ppermute | solution.py:243
  19.6 17.4 %all-to-all-start = ((bf16[64,2,896]{2,1,0:T(2,128)(2,1)}), bf16[64,2,896]{2,1,0:T(2,128)(2,1)S(1)}, u32[]{:S(2)}, u32[]{:S(2)}) async-start(bf16[64,2,896]{2,1,0:T(2,128)(2,1)} %shard_map.114), calls=%async_computation | async-start | bytes 458752 | tf_op jit(solution)/shard_map/all_to_all | solution.py:262
  37.0 0.0 copy-start.2
  37.0 0.0 copy-start.5
  37.0 0.0 copy-start.3
  37.0 4.5 %collective-permute-start.3 = (bf16[16,4096]{1,0:T(8,128)(2,1)S(1)}, bf16[16,4096]{1,0:T(8,128)(2,1)S(1)}, u32[]{:S(2)}, u32[]{:S(2)}) collective-permute-start(bf16[16,4096]{1,0:T(8,128)(2,1)S(1)} %shard_map.116.refs_8_), channel_id=1, source_target_pairs={{0,6},{1,7},{2,4},{3,5},{4,2},{5,3},{6,0},{7,1},{8,14},{9,15},{10,... | collective-permute-start | bytes 393224 | tf_op jit(solution)/shard_map/ppermute | solution.py:261
  41.6 0.0 copy-start.8
  41.6 0.0 copy-done.2
  41.6 0.0 copy-done.5
  41.6 0.0 copy-done.3
  41.6 0.6 %copy-done.8 = s32[32]{0:T(128)S(1)} copy-done((s32[32]{0:T(128)S(1)}, s32[32]{0:T(128)}, u32[]{:S(2)}) %copy-start.8) | copy-done | bytes 152
  42.2 1.1 %shard_map.115 = (f32[32,512]{1,0:T(8,128)S(1)}, f32[32,512]{1,0:T(8,128)S(1)}, f32[256,128]{1,0:T(8,128)S(1)}) custom-call(s32[32]{0:T(128)S(1)} %copy-done.8, bf16[1,512]{1,0:T(2,128)(2,1)S(1)} %copy-done.7, bf16[32,512]{1,0:T(8,128)(2,1)S(1)} %copy-done.5, bf16[512,128]{1,0:T(8,128)(2,1)S(1)} %copy-done.2, f32[8,512]{1,0:T(8,128)S(1)} %copy-done.3), custom_call_target="tpu_custom_call" | custom-call | flops 33554432 | bytes 524288 | tf_op jit(solution)/shard_map/pallas_call | solution.py:16
  43.3 0.0 all-to-all-done.refs_2_.refs_1_
  43.3 0.9 %shard_map.118 = f32[8,8,144]{2,1,0:T(8,128)} custom-call(s32[1]{0:T(128)S(6)} %select_n.23.refs_0_, bf16[64,2,896]{2,1,0:T(2,128)(2,1)S(1)} %all-to-all-done.refs_2_.refs_1_), custom_call_target="tpu_custom_call" | custom-call | bytes 458752 | tf_op jit(solution)/shard_map/pallas_call | solution.py:16
  44.3 0.0 copy-start.6
  44.3 7.0 %all-to-all-start.1 = ((f32[8,8,144]{2,1,0:T(8,128)}), f32[8,8,144]{2,1,0:T(8,128)S(1)}, u32[]{:S(2)}, u32[]{:S(2)}) async-start(f32[8,8,144]{2,1,0:T(8,128)} %shard_map.118), calls=%async_computation.1 | async-start | bytes 131072 | tf_op jit(solution)/shard_map/all_to_all | solution.py:297
  51.2 0.0 collective-permute-done.3.refs_9_
  51.2 0.0 copy-done.6
  51.2 2.0 %shard_map.117 = (f32[8,32]{1,0:T(8,128)}, f32[8,32]{1,0:T(8,128)S(1)}, bf16[8,4096]{1,0:T(8,128)(2,1)}) custom-call(s32[32]{0:T(128)S(1)} %copy-done.8, s32[1]{0:T(128)S(6)} %select_n.20.refs_1_, bf16[64,2,896]{2,1,0:T(2,128)(2,1)S(1)} %all-to-all-done.refs_2_.refs_1_, f32[32,512]{1,0:T(8,128)S(1)} %get-tuple-element.35.refs_3_, ...), custom_call_target="tpu_custom_call" | custom-call | flops 2097152 | bytes 524288 | tf_op jit(solution)/shard_map/pallas_call | solution.py:16
  53.3 0.2 all-to-all-done.1.refs_3_
  53.5 0.7 %shard_map.119 = (f32[4,144]{1,0:T(4,128)}, f32[8,144]{1,0:T(8,128)}) custom-call(s32[1]{0:T(128)S(6)} %select_n.21.side_ref.odd_ref.refs_0_, s32[1]{0:T(128)S(6)} %select_n.20.refs_1_, f32[8,32]{1,0:T(8,128)S(1)} %get-tuple-element.41.refs_2_, f32[8,8,144]{2,1,0:T(8,128)S(1)} %all-to-all-done.1.refs_3_), custom_call_target="tpu_custom_call" | custom-call | bytes 32768 | tf_op jit(solution)/shard_map/pallas_call | solution.py:16
  (3 shorter events, 0.1 us)
Async XLA Ops:
  0.6 1.1 %copy-start = (bf16[96,4096]{1,0:T(8,128)(2,1)S(1)}, bf16[96,4096]{1,0:T(8,128)(2,1)}, u32[]{:S(2)}) copy-start(bf16[96,4096]{1,0:T(8,128)(2,1)} %refs_1_.3) | copy-start | bytes 2359300
  1.8 1.5 %copy-start.4 = (bf16[4,4096]{1,0:T(4,128)(2,1)S(1)}, bf16[4,4096]{1,0:T(4,128)(2,1)}, u32[]{:S(2)}) copy-start(bf16[4,4096]{1,0:T(4,128)(2,1)} %own_ref.1) | copy-start | bytes 98308
  1.8 10.3 %copy-start.1 = (bf16[96,4096]{1,0:T(8,128)(2,1)S(1)}, bf16[96,4096]{1,0:T(8,128)(2,1)}, u32[]{:S(2)}) copy-start(bf16[96,4096]{1,0:T(8,128)(2,1)} %refs_1_.3) | copy-start | bytes 2359300
  1.8 14.1 %collective-permute-start = (bf16[96,2048]{1,0:T(8,128)(2,1)S(1)}, bf16[96,2048]{1,0:T(8,128)(2,1)S(1)}, u32[]{:S(2)}, u32[]{:S(2)}) collective-permute-start(bf16[96,2048]{1,0:T(8,128)(2,1)S(1)} %shard_map.111), channel_id=1, source_target_pairs={{8,0},{16,8},{24,16},{32,24},{40,32},{48,40},{56,48},{64,56},{72,6... | collective-permute-start | bytes 1179656 | tf_op jit(solution)/shard_map/ppermute | solution.py:225
  3.3 10.7 %collective-permute-start.1 = (bf16[4,4096]{1,0:T(4,128)(2,1)S(1)}, bf16[4,4096]{1,0:T(4,128)(2,1)S(1)}, u32[]{:S(2)}, u32[]{:S(2)}) collective-permute-start(bf16[4,4096]{1,0:T(4,128)(2,1)S(1)} %copy-done.4), channel_id=1, source_target_pairs={{0,1},{1,0},{2,3},{3,2},{4,5},{5,4},{6,7},{7,6},{8,9},{9,8},{10,11... | collective-permute-start | bytes 98312 | tf_op jit(solution)/shard_map/ppermute | solution.py:226
  13.9 2.0 %copy-start.7 = (bf16[1,512]{1,0:T(2,128)(2,1)S(1)}, bf16[1,512]{1,0:T(2,128)(2,1)}, u32[]{:S(2)}) copy-start(bf16[1,512]{1,0:T(2,128)(2,1)} %x_ref.1) | copy-start | bytes 3076
  14.0 5.6 %collective-permute-start.2 = (bf16[8,4096]{1,0:T(8,128)(2,1)S(1)}, bf16[8,4096]{1,0:T(8,128)(2,1)S(1)}, u32[]{:S(2)}, u32[]{:S(2)}) collective-permute-start(bf16[8,4096]{1,0:T(8,128)(2,1)S(1)} %shard_map.113.refs_3_.own_ref), channel_id=1, source_target_pairs={{0,2},{1,3},{2,0},{3,1},{4,6},{5,7},{6,4},{7,5},{8,10},{9,11},{10,... | collective-permute-start | bytes 196616 | tf_op jit(solution)/shard_map/ppermute | solution.py:243
  19.6 23.8 %all-to-all-start = ((bf16[64,2,896]{2,1,0:T(2,128)(2,1)}), bf16[64,2,896]{2,1,0:T(2,128)(2,1)S(1)}, u32[]{:S(2)}, u32[]{:S(2)}) async-start(bf16[64,2,896]{2,1,0:T(2,128)(2,1)} %shard_map.114), calls=%async_computation | async-start | bytes 458752 | tf_op jit(solution)/shard_map/all_to_all | solution.py:262
  37.0 4.6 %copy-start.2 = (bf16[512,128]{1,0:T(8,128)(2,1)S(1)}, bf16[512,128]{1,0:T(8,128)(2,1)}, u32[]{:S(2)}) copy-start(bf16[512,128]{1,0:T(8,128)(2,1)} %z_ref.1) | copy-start | bytes 393220
  37.0 4.6 %copy-start.5 = (bf16[32,512]{1,0:T(8,128)(2,1)S(1)}, bf16[32,512]{1,0:T(8,128)(2,1)}, u32[]{:S(2)}) copy-start(bf16[32,512]{1,0:T(8,128)(2,1)} %y_ref.1) | copy-start | bytes 98308
  37.0 4.6 %copy-start.3 = (f32[8,512]{1,0:T(8,128)S(1)}, f32[8,512]{1,0:T(8,128)}, u32[]{:S(2)}) copy-start(f32[8,512]{1,0:T(8,128)} %refs_6_.1) | copy-start | bytes 49156
  37.0 14.2 %collective-permute-start.3 = (bf16[16,4096]{1,0:T(8,128)(2,1)S(1)}, bf16[16,4096]{1,0:T(8,128)(2,1)S(1)}, u32[]{:S(2)}, u32[]{:S(2)}) collective-permute-start(bf16[16,4096]{1,0:T(8,128)(2,1)S(1)} %shard_map.116.refs_8_), channel_id=1, source_target_pairs={{0,6},{1,7},{2,4},{3,5},{4,2},{5,3},{6,0},{7,1},{8,14},{9,15},{10,... | collective-permute-start | bytes 393224 | tf_op jit(solution)/shard_map/ppermute | solution.py:261
  41.6 0.7 %copy-start.8 = (s32[32]{0:T(128)S(1)}, s32[32]{0:T(128)}, u32[]{:S(2)}) copy-start(s32[32]{0:T(128)} %refs_0_.3) | copy-start | bytes 388
  44.3 7.0 %copy-start.6 = (f32[32,32]{1,0:T(8,128)S(1)}, f32[32,32]{1,0:T(8,128)}, u32[]{:S(2)}) copy-start(f32[32,32]{1,0:T(8,128)} %refs_7_.1) | copy-start | bytes 12292
  44.3 9.2 %all-to-all-start.1 = ((f32[8,8,144]{2,1,0:T(8,128)}), f32[8,8,144]{2,1,0:T(8,128)S(1)}, u32[]{:S(2)}, u32[]{:S(2)}) async-start(f32[8,8,144]{2,1,0:T(8,128)} %shard_map.118), calls=%async_computation.1 | async-start | bytes 131072 | tf_op jit(solution)/shard_map/all_to_all | solution.py:297

commit v4 on v3

--- a/solution.py
+++ b/solution.py
@@ -99,39 +99,36 @@
     out_ref[...] = jnp.concatenate([first, second], 0).astype(BF16)
 
 
-def field(
-    cells_ref, x_ref, y_ref, z_ref, coefficients_ref, at_y_ref, at_z_ref, conductivity_ref, pick_z, wide_y
-):
-    width_y, width_z = y_ref.shape[0], z_ref.shape[1]
-    plane = width_y * width_z
-    wide_y[...] = y_ref[...].astype(F32)
-    lanes = lax.broadcasted_iota(jnp.int32, (1, width_z), 1)
-    for q in range(cells_ref.shape[0]):
-        cell = cells_ref[q]
-        at_y_ref[q : q + 1] = wide_y[pl.ds((cell % plane) // width_z, 1), :]
-        pick_z[q : q + 1] = jnp.where(lanes == cell % width_z, 1.0, 0.0)
-    at_z_ref[...] = lax.dot_general(
-        pick_z[...].astype(BF16), z_ref[...], (((1,), (1,)), ((), ())), preferred_element_type=F32
-    )
+def field(x_ref, y_ref, z_ref, coefficients_ref, conductivity_ref):
+    wide_y = y_ref[...].astype(F32)
     scaled = x_ref[...].astype(F32) * coefficients_ref[...]
-    left = [(scaled * wide_y[y : y + 1]).astype(BF16) for y in range(width_y)]
+    left = [(scaled * wide_y[y : y + 1]).astype(BF16) for y in range(wide_y.shape[0])]
     logs = jnp.dot(jnp.concatenate(left, 0), z_ref[...], preferred_element_type=F32)
     conductivity_ref[...] = jnp.exp(logs)
 
 
 def interpolation(
-    meet, plane, cells_ref, chip_ref, arrived_ref, at_y_ref, at_z_ref, conductivity_ref,
-    coefficients_ref, inverse_ref, near_eim_ref, far_eim_ref, turned_ref, kept_ref, error_ref, pick_x,
+    meet, plane, cells_ref, chip_ref, arrived_ref, y_ref, z_ref, conductivity_ref,
+    coefficients_ref, inverse_ref, near_eim_ref, far_eim_ref, turned_ref, kept_ref, error_ref,
+    pick_x, pick_y, pick_z, wide_y,
 ):
     points, modes = pick_x.shape
     slabs = arrived_ref.shape[0]
     snaps = coefficients_ref.shape[0]
     width_z = conductivity_ref.shape[1]
     gram_width = arrived_ref.shape[2] - modes
+    wide_y[...] = y_ref[...].astype(F32)
+    lanes = lax.broadcasted_iota(jnp.int32, (1, width_z), 1)
     for q in range(points):
-        slab = (cells_ref[q] // plane + slabs - meet) % slabs
+        cell = cells_ref[q]
+        slab = (cell // plane + slabs - meet) % slabs
         pick_x[q : q + 1] = arrived_ref[slab][:, gram_width:].astype(F32)[1:2]
-    at_x, at_y, at_z = pick_x[...], at_y_ref[...], at_z_ref[...]
+        pick_y[q : q + 1] = wide_y[pl.ds((cell % plane) // width_z, 1), :]
+        pick_z[q : q + 1] = jnp.where(lanes == cell % width_z, 1.0, 0.0)
+    at_z = lax.dot_general(
+        pick_z[...].astype(BF16), z_ref[...], (((1,), (1,)), ((), ())), preferred_element_type=F32
+    )
+    at_x, at_y = pick_x[...], pick_y[...]
     coefficients = coefficients_ref[...]
     lane = lax.broadcasted_iota(jnp.int32, (points, 128), 1)
     logs = jnp.zeros((points, 128), F32)
@@ -260,29 +257,26 @@
     )
     eim_far = lax.ppermute(eim_near, term, [(i, i ^ (groups - 2)) for i in range(groups)])
     arrived = lax.all_to_all(packed, space, 0, 0, axis_index_groups=[ranks], tiled=True)
-    at_y, at_z, conductivity = call(
+    conductivity = call(
         field,
-        (
-            shape((points, modes), F32),
-            shape((points, modes), F32),
-            shape((width_y * snaps, width_z), F32),
-        ),
-        (magic_cells, x_modes, y_modes, z_modes, factors),
-        specs=[SMEM] + [VMEM] * 4,
-        scratch=[pltpu.VMEM((points, width_z), F32), pltpu.VMEM((width_y, modes), F32)],
+        shape((width_y * snaps, width_z), F32),
+        (x_modes, y_modes, z_modes, factors),
         flops=2 * snaps * width_y * modes * width_z,
         moved=4 * points * cells,
     )
-    arrived, at_y, at_z, conductivity = lax.optimization_barrier(
-        (arrived, at_y, at_z, conductivity)
-    )
+    arrived, conductivity = lax.optimization_barrier((arrived, conductivity))
     eim_turned, turned, interp_error = call(
         lambda *refs: interpolation(meet, cells, *refs),
         (shape((snaps, points), F32), shape((snaps, points), F32), shape((snaps, cells), BF16)),
-        (magic_cells, chip, arrived, at_y, at_z, conductivity, coefficients, interp_inverse)
+        (magic_cells, chip, arrived, y_modes, z_modes, conductivity, coefficients, interp_inverse)
         + (eim_near, eim_far),
         specs=[SMEM] * 2 + [VMEM] * 8,
-        scratch=[pltpu.VMEM((points, modes), F32)],
+        scratch=[
+            pltpu.VMEM((points, modes), F32),
+            pltpu.VMEM((points, modes), F32),
+            pltpu.VMEM((points, width_z), F32),
+            pltpu.VMEM((width_y, modes), F32),
+        ],
         flops=2 * snaps * points * cells,
         moved=4 * points * cells,
     )

time: 54.6 us -> 54.4 us (level)
  starting transfers between devices: 41 us -> 42.1 us
  local copies, waits for them, and re-layouts: 1.78 us -> 1.17 us
    all_to_all x1, starting transfers between devices: 6.97 us -> 8.06 us  [local(): lax.all_to_all(spread, term, 0, 0, axis_index_groups=[term_ranks], tiled=...]
    unnamed x18, local copies, waits for them, and re-layouts: 1.78 us -> 1.17 us
  transfers between devices with their start and end apart: 6 -> 6, of which waited for: 2 -> 1; matrix products, arithmetic and copies ran while one was open for 0% -> 0% of each run, Pallas kernels for 14% -> 13%
where the time goes in v4:
time: 54.4 us; the launch traced here: 53.9 us
  starting transfers between devices  42.1 us (77%)
  Pallas kernels  7.99 us (15%)
  waiting for transfers between devices  1.83 us (3%)
  local copies, waits for them, and re-layouts  1.17 us (2%)
  between operations  0.88 us (2%)
    all_to_all x1, starting transfers between devices, local(): lax.all_to_all(packed, space, 0, 0, axis_index_groups=[ranks], tiled=True)  17.4 us
    ppermute x1, starting transfers between devices, local(): eim_other = lax.ppermute(eim_basis, term, swap)  8.79 us
    all_to_all x1, starting transfers between devices, local(): lax.all_to_all(spread, term, 0, 0, axis_index_groups=[term_ranks], tiled=...  8.06 us
    pallas_call x8, Pallas kernels, call(): pl.pallas_call(body, out_shape=out_shape, in_specs=specs or [VMEM] * len(...  7.97 us
    ppermute x1, starting transfers between devices, local(): lax.ppermute(eim_near, term, [(i, i ^ groups - 2) for i in range(groups)])  4.51 us
    ppermute x1, starting transfers between devices, local(): lax.ppermute(eim_pair, term, [(i, i ^ 2) for i in range(groups)])  1.92 us
    ppermute x1, waiting for transfers between devices, local(): lax.ppermute(eim_pair, term, [(i, i ^ 2) for i in range(groups)])  1.82 us
    ppermute x1, starting transfers between devices, local(): near = lax.ppermute(mine, space, [(i + 1, i) for i in range(slabs - 1)])  1.42 us
  transfers between devices with their start and end apart: 6, of which 1 were waited for; matrix products, arithmetic and copies ran while one was open for 0% of the time, Pallas kernels for 13%

profile of v4, /device:TPU:1, one launch (start us, length us, event | category | flops | bytes accessed | tf_op | source)
XLA Modules:
  0.0 53.9 jit_solution(5635176583041577096)
XLA Ops:
  0.6 0.0 copy-start
  0.7 1.1 %copy-done = bf16[96,4096]{1,0:T(8,128)(2,1)S(1)} copy-done((bf16[96,4096]{1,0:T(8,128)(2,1)S(1)}, bf16[96,4096]{1,0:T(8,128)(2,1)}, u32[]{:S(2)}) %copy-start) | copy-done | bytes 786456
  1.8 0.0 copy-start.5
  1.8 0.0 copy-start.1
  1.8 1.4 %collective-permute-start = (bf16[96,2048]{1,0:T(8,128)(2,1)S(1)}, bf16[96,2048]{1,0:T(8,128)(2,1)S(1)}, u32[]{:S(2)}, u32[]{:S(2)}) collective-permute-start(bf16[96,2048]{1,0:T(8,128)(2,1)S(1)} %shard_map.111), channel_id=1, source_target_pairs={{8,0},{16,8},{24,16},{32,24},{40,32},{48,40},{56,48},{64,56},{72,6... | collective-permute-start | bytes 1179656 | tf_op jit(solution)/shard_map/ppermute | solution.py:222
  3.2 0.0 copy-done.5
  3.3 8.8 %collective-permute-start.1 = (bf16[4,4096]{1,0:T(4,128)(2,1)S(1)}, bf16[4,4096]{1,0:T(4,128)(2,1)S(1)}, u32[]{:S(2)}, u32[]{:S(2)}) collective-permute-start(bf16[4,4096]{1,0:T(4,128)(2,1)S(1)} %copy-done.5), channel_id=1, source_target_pairs={{0,1},{1,0},{2,3},{3,2},{4,5},{5,4},{6,7},{7,6},{8,9},{9,8},{10,11... | collective-permute-start | bytes 98312 | tf_op jit(solution)/shard_map/ppermute | solution.py:223
  12.0 0.0 copy-done.1
  12.1 1.8 %shard_map.112.refs_4_ = f32[384,96]{1,0:T(8,128)S(1)} custom-call(bf16[96,4096]{1,0:T(8,128)(2,1)S(1)} %copy-done.1, bf16[4,4096]{1,0:T(4,128)(2,1)S(1)} %copy-done.5), custom_call_target="tpu_custom_call" | custom-call | flops 603979776 | bytes 786432 | tf_op jit(solution)/shard_map/pallas_call | solution.py:16
  13.9 0.0 copy-start.7
  13.9 0.0 collective-permute-done.1.other_ref
  14.0 1.9 %collective-permute-start.2 = (bf16[8,4096]{1,0:T(8,128)(2,1)S(1)}, bf16[8,4096]{1,0:T(8,128)(2,1)S(1)}, u32[]{:S(2)}, u32[]{:S(2)}) collective-permute-start(bf16[8,4096]{1,0:T(8,128)(2,1)S(1)} %shard_map.113.refs_3_.own_ref), channel_id=1, source_target_pairs={{0,2},{1,3},{2,0},{3,1},{4,6},{5,7},{6,4},{7,5},{8,10},{9,11},{10,... | collective-permute-start | bytes 196616 | tf_op jit(solution)/shard_map/ppermute | solution.py:240
  15.9 0.0 collective-permute-done.refs_2_
  15.9 0.0 copy-done.7
  15.9 1.8 %shard_map.114 = bf16[64,2,896]{2,1,0:T(2,128)(2,1)} custom-call(s32[1]{0:T(128)S(6)} %select_n.21.side_ref.odd_ref.refs_0_, bf16[96,4096]{1,0:T(8,128)(2,1)S(1)} %copy-done.1, bf16[96,2048]{1,0:T(8,128)(2,1)S(1)} %collective-permute-done.refs_2_, bf16[8,4096]{1,0:T(8,128)(2,1)S(1)} %shard_map.113.refs_3_.own_ref, f32[384,96]{1,0:T(8,128)S(1)} %shard_map.112.refs_4_, ...), custom_call_target="tpu_custom_call" | custom-call | flops 301989888 | bytes 1572864 | tf_op jit(solution)/shard_map/pallas_call | solution.py:16
  17.7 1.8 %collective-permute-done.2.other_ref = bf16[8,4096]{1,0:T(8,128)(2,1)S(1)} collective-permute-done((bf16[8,4096]{1,0:T(8,128)(2,1)S(1)}, bf16[8,4096]{1,0:T(8,128)(2,1)S(1)}, u32[]{:S(2)}, u32[]{:S(2)}) %collective-permute-start.2) | collective-permute-done | bytes 65568 | tf_op jit(solution)/shard_map/ppermute | solution.py:240
  19.6 17.4 %all-to-all-start = ((bf16[64,2,896]{2,1,0:T(2,128)(2,1)}), bf16[64,2,896]{2,1,0:T(2,128)(2,1)S(1)}, u32[]{:S(2)}, u32[]{:S(2)}) async-start(bf16[64,2,896]{2,1,0:T(2,128)(2,1)} %shard_map.114), calls=%async_computation | async-start | bytes 458752 | tf_op jit(solution)/shard_map/all_to_all | solution.py:259
  37.0 0.0 copy-start.2
  37.0 0.0 copy-start.3
  37.0 0.0 copy-start.4
  37.1 4.5 %collective-permute-start.3 = (bf16[16,4096]{1,0:T(8,128)(2,1)S(1)}, bf16[16,4096]{1,0:T(8,128)(2,1)S(1)}, u32[]{:S(2)}, u32[]{:S(2)}) collective-permute-start(bf16[16,4096]{1,0:T(8,128)(2,1)S(1)} %shard_map.116.refs_8_), channel_id=1, source_target_pairs={{0,6},{1,7},{2,4},{3,5},{4,2},{5,3},{6,0},{7,1},{8,14},{9,15},{10,... | collective-permute-start | bytes 393224 | tf_op jit(solution)/shard_map/ppermute | solution.py:258
  41.6 0.0 copy-done.2
  41.6 0.0 copy-done.3
  41.6 0.0 copy-done.4
  41.6 0.2 shard_map.115.refs_5_
  41.9 0.0 all-to-all-done.refs_2_.refs_1_
  41.9 0.9 %shard_map.118 = f32[8,8,144]{2,1,0:T(8,128)} custom-call(s32[1]{0:T(128)S(6)} %select_n.23.refs_0_, bf16[64,2,896]{2,1,0:T(2,128)(2,1)S(1)} %all-to-all-done.refs_2_.refs_1_), custom_call_target="tpu_custom_call" | custom-call | bytes 458752 | tf_op jit(solution)/shard_map/pallas_call | solution.py:16
  42.8 0.0 copy-start.6
  42.8 0.0 copy-start.8
  42.8 8.1 %all-to-all-start.1 = ((f32[8,8,144]{2,1,0:T(8,128)}), f32[8,8,144]{2,1,0:T(8,128)S(1)}, u32[]{:S(2)}, u32[]{:S(2)}) async-start(f32[8,8,144]{2,1,0:T(8,128)} %shard_map.118), calls=%async_computation.1 | async-start | bytes 131072 | tf_op jit(solution)/shard_map/all_to_all | solution.py:291
  50.9 0.0 collective-permute-done.3.refs_9_
  50.9 0.0 copy-done.6
  50.9 0.0 copy-done.8
  50.9 2.3 %shard_map.117 = (f32[8,32]{1,0:T(8,128)}, f32[8,32]{1,0:T(8,128)S(1)}, bf16[8,4096]{1,0:T(8,128)(2,1)}) custom-call(s32[32]{0:T(128)S(1)} %copy-done.8, s32[1]{0:T(128)S(6)} %select_n.20.refs_1_, bf16[64,2,896]{2,1,0:T(2,128)(2,1)S(1)} %all-to-all-done.refs_2_.refs_1_, bf16[32,512]{1,0:T(8,128)(2,1)S(1)} %copy-done.3, bf16[512,128]{1,0:T(8,128)(2,1)S(1)} %copy-done.2, ...), custom_call_target="tpu_custom_call" | custom-call | flops 2097152 | bytes 524288 | tf_op jit(solution)/shard_map/pallas_call | solution.py:16
  53.2 0.0 all-to-all-done.1.refs_3_
  53.2 0.7 %shard_map.119 = (f32[4,144]{1,0:T(4,128)}, f32[8,144]{1,0:T(8,128)}) custom-call(s32[1]{0:T(128)S(6)} %select_n.21.side_ref.odd_ref.refs_0_, s32[1]{0:T(128)S(6)} %select_n.20.refs_1_, f32[8,32]{1,0:T(8,128)S(1)} %get-tuple-element.31.refs_2_, f32[8,8,144]{2,1,0:T(8,128)S(1)} %all-to-all-done.1.refs_3_), custom_call_target="tpu_custom_call" | custom-call | bytes 32768 | tf_op jit(solution)/shard_map/pallas_call | solution.py:16
  (3 shorter events, 0.1 us)
Async XLA Ops:
  0.6 1.1 %copy-start = (bf16[96,4096]{1,0:T(8,128)(2,1)S(1)}, bf16[96,4096]{1,0:T(8,128)(2,1)}, u32[]{:S(2)}) copy-start(bf16[96,4096]{1,0:T(8,128)(2,1)} %refs_1_.3) | copy-start | bytes 2359300
  1.8 1.5 %copy-start.5 = (bf16[4,4096]{1,0:T(4,128)(2,1)S(1)}, bf16[4,4096]{1,0:T(4,128)(2,1)}, u32[]{:S(2)}) copy-start(bf16[4,4096]{1,0:T(4,128)(2,1)} %own_ref.1) | copy-start | bytes 98308
  1.8 10.3 %copy-start.1 = (bf16[96,4096]{1,0:T(8,128)(2,1)S(1)}, bf16[96,4096]{1,0:T(8,128)(2,1)}, u32[]{:S(2)}) copy-start(bf16[96,4096]{1,0:T(8,128)(2,1)} %refs_1_.3) | copy-start | bytes 2359300
  1.8 14.1 %collective-permute-start = (bf16[96,2048]{1,0:T(8,128)(2,1)S(1)}, bf16[96,2048]{1,0:T(8,128)(2,1)S(1)}, u32[]{:S(2)}, u32[]{:S(2)}) collective-permute-start(bf16[96,2048]{1,0:T(8,128)(2,1)S(1)} %shard_map.111), channel_id=1, source_target_pairs={{8,0},{16,8},{24,16},{32,24},{40,32},{48,40},{56,48},{64,56},{72,6... | collective-permute-start | bytes 1179656 | tf_op jit(solution)/shard_map/ppermute | solution.py:222
  3.3 10.7 %collective-permute-start.1 = (bf16[4,4096]{1,0:T(4,128)(2,1)S(1)}, bf16[4,4096]{1,0:T(4,128)(2,1)S(1)}, u32[]{:S(2)}, u32[]{:S(2)}) collective-permute-start(bf16[4,4096]{1,0:T(4,128)(2,1)S(1)} %copy-done.5), channel_id=1, source_target_pairs={{0,1},{1,0},{2,3},{3,2},{4,5},{5,4},{6,7},{7,6},{8,9},{9,8},{10,11... | collective-permute-start | bytes 98312 | tf_op jit(solution)/shard_map/ppermute | solution.py:223
  13.9 2.0 %copy-start.7 = (bf16[1,512]{1,0:T(2,128)(2,1)S(1)}, bf16[1,512]{1,0:T(2,128)(2,1)}, u32[]{:S(2)}) copy-start(bf16[1,512]{1,0:T(2,128)(2,1)} %x_ref.1) | copy-start | bytes 3076
  14.0 5.6 %collective-permute-start.2 = (bf16[8,4096]{1,0:T(8,128)(2,1)S(1)}, bf16[8,4096]{1,0:T(8,128)(2,1)S(1)}, u32[]{:S(2)}, u32[]{:S(2)}) collective-permute-start(bf16[8,4096]{1,0:T(8,128)(2,1)S(1)} %shard_map.113.refs_3_.own_ref), channel_id=1, source_target_pairs={{0,2},{1,3},{2,0},{3,1},{4,6},{5,7},{6,4},{7,5},{8,10},{9,11},{10,... | collective-permute-start | bytes 196616 | tf_op jit(solution)/shard_map/ppermute | solution.py:240
  19.6 22.3 %all-to-all-start = ((bf16[64,2,896]{2,1,0:T(2,128)(2,1)}), bf16[64,2,896]{2,1,0:T(2,128)(2,1)S(1)}, u32[]{:S(2)}, u32[]{:S(2)}) async-start(bf16[64,2,896]{2,1,0:T(2,128)(2,1)} %shard_map.114), calls=%async_computation | async-start | bytes 458752 | tf_op jit(solution)/shard_map/all_to_all | solution.py:259
  37.0 4.6 %copy-start.2 = (bf16[512,128]{1,0:T(8,128)(2,1)S(1)}, bf16[512,128]{1,0:T(8,128)(2,1)}, u32[]{:S(2)}) copy-start(bf16[512,128]{1,0:T(8,128)(2,1)} %refs_4_.1) | copy-start | bytes 393220
  37.0 4.6 %copy-start.3 = (bf16[32,512]{1,0:T(8,128)(2,1)S(1)}, bf16[32,512]{1,0:T(8,128)(2,1)}, u32[]{:S(2)}) copy-start(bf16[32,512]{1,0:T(8,128)(2,1)} %refs_3_.1) | copy-start | bytes 98308
  37.0 4.6 %copy-start.4 = (f32[8,512]{1,0:T(8,128)S(1)}, f32[8,512]{1,0:T(8,128)}, u32[]{:S(2)}) copy-start(f32[8,512]{1,0:T(8,128)} %refs_6_.1) | copy-start | bytes 49156
  37.1 13.8 %collective-permute-start.3 = (bf16[16,4096]{1,0:T(8,128)(2,1)S(1)}, bf16[16,4096]{1,0:T(8,128)(2,1)S(1)}, u32[]{:S(2)}, u32[]{:S(2)}) collective-permute-start(bf16[16,4096]{1,0:T(8,128)(2,1)S(1)} %shard_map.116.refs_8_), channel_id=1, source_target_pairs={{0,6},{1,7},{2,4},{3,5},{4,2},{5,3},{6,0},{7,1},{8,14},{9,15},{10,... | collective-permute-start | bytes 393224 | tf_op jit(solution)/shard_map/ppermute | solution.py:258
  42.8 8.1 %copy-start.6 = (f32[32,32]{1,0:T(8,128)S(1)}, f32[32,32]{1,0:T(8,128)}, u32[]{:S(2)}) copy-start(f32[32,32]{1,0:T(8,128)} %refs_7_.1) | copy-start | bytes 12292
  42.8 8.1 %copy-start.8 = (s32[32]{0:T(128)S(1)}, s32[32]{0:T(128)}, u32[]{:S(2)}) copy-start(s32[32]{0:T(128)} %refs_0_.3) | copy-start | bytes 388
  42.8 10.4 %all-to-all-start.1 = ((f32[8,8,144]{2,1,0:T(8,128)}), f32[8,8,144]{2,1,0:T(8,128)S(1)}, u32[]{:S(2)}, u32[]{:S(2)}) async-start(f32[8,8,144]{2,1,0:T(8,128)} %shard_map.118), calls=%async_computation.1 | async-start | bytes 131072 | tf_op jit(solution)/shard_map/all_to_all | solution.py:291
